TPU v7x, 512 devices: a whole 4x4x16 slice. The times are simulated.
512 devices in a mesh: dom: 128 (over x, z, core), sub: 4 (over y).
Axes of the slice: x: 4, y: 4, z: 16, core: 2. Of those that a mesh axis runs over, the one named last changes fastest.
Arguments:
- features: bfloat16 [524288, 256], P(('dom', 'sub')), may hold values from -16 to 16
- weight: bfloat16 [256, 256], replicated, may hold values from -0.375 to 0.375
- send_far: int32 [262144], P(('dom', 'sub')), may hold values from 0 to 1023
- send_near: int32 [65536], P(('dom', 'sub')), may hold values from 0 to 1023
- tile_dst: int32 [8192], P(('dom', 'sub')), may hold values from 0 to 7
- inner_src: int32 [4096], P(('dom', 'sub')), may hold values from 0 to 7
- outer_src: int32 [4096], P(('dom', 'sub')), may hold values from 0 to 4
- tile_live: int32 [512, 2], P(('dom', 'sub')), may hold values from 4 to 8
- tile_weight: bfloat16 [8192, 128, 128], P(('dom', 'sub')), may hold values from -0.3125 to 0.3125
Outputs:
- whitened: bfloat16 [524288, 256], P(('dom', 'sub'))
- loss_value: float32 [], replicated
Inputs may be any that keep to these rules, and one draw needn't show every extreme that they name: `send_far`: rows may repeat. `tile_live`: live slots come first in each half of a device's slots.
All inputs are finite; a program needn't handle non-finite values.
Results may differ from a plain program's by a relative error of at most 0.0085.
Values may be sent and summed in bfloat16 or wider, within the bound.
No kernel may reach another device: no remote copies, remote signals or barrier semaphores. Data moves between devices by JAX's collectives and lax.ppermute only.
A program may use at most 64 MiB of HBM per device.

v0:
```python
import jax
import jax.numpy as jnp
from jax import lax
from jax.sharding import Mesh
from jax.sharding import PartitionSpec as P

DOM = ("dom_0", "dom_1", "dom_2")
DOM_SUB = ("dom_0", "dom_1", "dom_2", "sub")


epsilon = 1e-05


def padded_to(lines, size):
    spare = -len(lines) % size
    return jnp.pad(lines, [(0, spare)] + [(0, 0)] * (lines.ndim - 1))


def sent_to_all(value, axis):
    size = lax.axis_size(axis)
    return lax.all_to_all(
        jnp.broadcast_to(value[None], (size, *value.shape)), axis, 0, 0, tiled=True
    )


def laid_out(pieces, dim):
    pieces = jnp.moveaxis(pieces, 0, dim)
    shape = pieces.shape
    return pieces.reshape(*shape[:dim], shape[dim] * shape[dim + 1], *shape[dim + 2 :])


def gathered_by_axis(value, axes, dim):
    far, near = axes
    initial = sent_to_all(value, far)
    pieces = jnp.swapaxes(sent_to_all(initial, near), 0, 1)
    return laid_out(pieces.reshape(-1, *value.shape), dim)


def cut_along(value, dim, size):
    shape = value.shape
    pieces = value.reshape(*shape[:dim], size, shape[dim] // size, *shape[dim + 1 :])
    return jnp.moveaxis(pieces, dim, 0)


def sum_at_owner(value, axis, dim):
    size = lax.axis_size(axis)
    pieces = lax.all_to_all(cut_along(value, dim, size), axis, 0, 0, tiled=True)
    return jnp.sum(pieces, axis=0)


def sum_by_axis(value, axes, dim):
    far, near = axes
    own = sum_at_owner(cut_along(value, dim, lax.axis_size(far)), near, dim + 1)
    return jnp.sum(lax.all_to_all(own, far, 0, 0, tiled=True), axis=0)


def nested_sum(value, axes):
    padded = padded_to(value, lax.axis_size(axes[0]) * lax.axis_size(axes[1]))
    whole = gathered_by_axis(sum_by_axis(padded, axes, 0), axes, 0)
    return lax.slice_in_dim(whole, 0, len(value)).reshape(value.shape)


def together(arrays, axis):
    ends = [0]
    for a in arrays:
        ends.append(ends[-1] + a.size)
    subtotal = nested_sum(jnp.concatenate([a.ravel() for a in arrays]), axis)
    return tuple((subtotal[b:e].reshape(a.shape) for a, b, e in zip(arrays, ends, ends[1:])))


def aggregate_tiles(slot_weights, source_tiles, dest_tiles, slot_mask, tile_table, local_tiles):
    selected = tile_table[source_tiles]
    products = jnp.einsum(
        "kij,kjf->kif", slot_weights, selected, preferred_element_type=jnp.float32
    )
    tile_index = jnp.arange(local_tiles, dtype=jnp.int32)
    selector = ((dest_tiles[None, :] == tile_index[:, None]) & slot_mask[None, :]).astype(
        jnp.float32
    )
    return jnp.einsum("tk,kif->tif", selector, products, precision=lax.Precision.HIGHEST)


def whiten_map(gram_sum, vertex_count, feat_width):
    identity = jnp.eye(feat_width, dtype=jnp.float32)
    scaled = gram_sum / vertex_count + epsilon * identity
    lower = jnp.linalg.cholesky(scaled)
    inverse = lax.linalg.triangular_solve(lower, identity, left_side=True, lower=True)
    return inverse.T


def apply_whitener(hidden, whitener):
    high_part = whitener.astype(jnp.bfloat16)
    low_part = (whitener - high_part.astype(jnp.float32)).astype(jnp.bfloat16)
    upper_term = jnp.dot(hidden, high_part, preferred_element_type=jnp.float32)
    lower_term = jnp.dot(hidden, low_part, preferred_element_type=jnp.float32)
    return upper_term + lower_term


def body(
    features, weight, send_far, send_near, tile_dst, inner_src, outer_src, tile_live, tile_weight
):
    row_count, feat_width = features.shape
    tile_size = tile_weight.shape[1]
    slot_count = inner_src.shape[0]
    local_tiles = row_count // tile_size
    own_table = features.reshape(local_tiles, tile_size, feat_width)
    slot_index = jnp.arange(slot_count, dtype=jnp.int32)
    inner_mask = slot_index < tile_live[0, 0]
    outer_mask = slot_index < tile_live[0, 1]
    far_rows = lax.all_to_all(features[send_far], DOM, split_axis=0, concat_axis=0, tiled=True)
    near_rows = lax.all_to_all(features[send_near], "sub", split_axis=0, concat_axis=0, tiled=True)
    halo_tiles = jnp.concatenate([far_rows, near_rows], 0).reshape(-1, tile_size, feat_width)
    tile_table = jnp.concatenate([own_table, halo_tiles], 0)
    source_tiles = jnp.concatenate([inner_src, outer_src + local_tiles])
    slot_mask = jnp.concatenate([inner_mask, outer_mask])
    summed = aggregate_tiles(
        tile_weight, source_tiles, tile_dst, slot_mask, tile_table, local_tiles
    )
    aggregate = summed.reshape(row_count, feat_width).astype(jnp.bfloat16)
    projected = jnp.dot(aggregate, weight, preferred_element_type=jnp.float32)
    features_f32 = features.astype(jnp.float32)
    hidden = (features_f32 + jax.nn.silu(projected)).astype(jnp.bfloat16)
    gram_part = lax.dot_general(
        hidden, hidden, (((0,), (0,)), ((), ())), preferred_element_type=jnp.float32
    )
    vertex_count = row_count * lax.axis_size(DOM) * lax.axis_size("sub")
    cross_part = lax.dot_general(
        hidden, features, (((0,), (0,)), ((), ())), preferred_element_type=jnp.float32
    )
    square_part = jnp.sum(features_f32 * features_f32)
    gram_sum, cross_sum, square_sum = together(
        (gram_part, cross_part, square_part), (("dom_0", "dom_1"), ("dom_2", "sub"))
    )
    whitener = whiten_map(gram_sum, vertex_count, feat_width)
    white = apply_whitener(hidden, whitener)
    gram_whitened = jnp.dot(gram_sum, whitener, precision=lax.Precision.HIGHEST)
    total_distance = (
        jnp.sum(whitener * gram_whitened) - 2.0 * jnp.sum(whitener * cross_sum) + square_sum
    )
    loss_value = total_distance / (vertex_count * feat_width)
    return (white.astype(jnp.bfloat16), loss_value)


def solution(mesh):
    torus = Mesh(
        mesh.devices.reshape(4, 16, 2, mesh.shape["sub"]), ("dom_0", "dom_1", "dom_2", "sub")
    )
    return jax.shard_map(
        body,
        mesh=torus,
        in_specs=(
            P(DOM_SUB, None),
            P(),
            P(DOM_SUB),
            P(DOM_SUB),
            P(DOM_SUB),
            P(DOM_SUB),
            P(DOM_SUB),
            P(DOM_SUB, None),
            P(DOM_SUB, None, None),
        ),
        out_specs=(P(DOM_SUB, None), P()),
        check_vma=False,
    )
```

profile of v0, /device:TPU:1, one launch (start us, length us, event | category | flops | bytes accessed | tf_op | source)
XLA Modules:
  0.0 218.4 jit_solution(8201363331453994282)
XLA Ops:
  1.5 2.7 %gather_fusion = bf16[512,256]{1,0:T(8,128)(2,1)S(1)} fusion(bf16[1024,256]{1,0:T(8,128)(2,1)} %param.9, s32[1024]{0:T(1024)S(1)} %pad_clamp_fusion.2), kind=kCustom, calls=%fused_computation | custom fusion | bytes 526336 | tf_op jit(solution)/shard_map/gather | solution.py:110
  4.9 20.4 %all-to-all-start = ((bf16[128,4,256]{2,1,0:T(4,128)(2,1)}), bf16[128,4,256]{2,1,0:T(4,128)(2,1)S(1)}, u32[]{:S(2)}, u32[]{:S(2)}) async-start(bf16[128,4,256]{2,1,0:T(4,128)(2,1)} %all_to_all.32), calls=%async_computation | async-start | bytes 524288 | tf_op jit(solution)/shard_map/all_to_all | solution.py:110
  25.4 1.5 gather_fusion.1
  27.5 1.3 iota_compare_fusion.6
  28.8 19.0 %all-to-all-done = bf16[128,4,256]{2,1,0:T(4,128)(2,1)S(1)} async-done(((bf16[128,4,256]{2,1,0:T(4,128)(2,1)}), bf16[128,4,256]{2,1,0:T(4,128)(2,1)S(1)}, u32[]{:S(2)}, u32[]{:S(2)}) %all-to-all-start) | async-done | bytes 262176 | tf_op jit(solution)/shard_map/all_to_all | solution.py:110
  47.8 4.2 %all-to-all-start.1 = ((bf16[4,32,256]{2,1,0:T(8,128)(2,1)}), bf16[4,32,256]{2,1,0:T(8,128)(2,1)S(1)}, u32[]{:S(2)}, u32[]{:S(2)}) async-start(bf16[4,32,256]{2,1,0:T(8,128)(2,1)} %bitcast.4), calls=%async_computation.1 | async-start | bytes 131072 | tf_op jit(solution)/shard_map/all_to_all | solution.py:111
  52.1 4.3 %all-to-all-done.1 = bf16[4,32,256]{2,1,0:T(8,128)(2,1)S(1)} async-done(((bf16[4,32,256]{2,1,0:T(8,128)(2,1)}), bf16[4,32,256]{2,1,0:T(8,128)(2,1)S(1)}, u32[]{:S(2)}, u32[]{:S(2)}) %all-to-all-start.1) | async-done | bytes 65568 | tf_op jit(solution)/shard_map/all_to_all | solution.py:111
  56.6 1.6 gather_fusion.2
  58.2 1.7 convolution_bitcast_fusion
  59.9 2.1 copy.40
  62.0 2.4 %convolution_convert_fusion = bf16[8,128,256]{2,0,1:T(8,128)(2,1)S(1)} fusion(f32[16,128,256]{2,0,1:T(8,128)} %copy.40, s32[16]{0:T(128)S(1)} %copy-done.4, pred[16]{0:T(512)(128)(4,1)S(1)} %pad_add_fusion), kind=kOutput, calls=%fused_computation.9 | convolution fusion | flops 50594048 | bytes 2621520 | tf_op jit(solution)/shard_map/tk,kif->tif/dot_general | solution.py:80
  64.5 1.1 fusion.2
  68.2 18.1 %all_to_all.49 = f32[8,64,257]{2,1,0:T(8,128)S(1)} all-to-all(f32[8,64,257]{2,1,0:T(8,128)S(1)} %copy.42), channel_id=1, replica_groups=mesh['dom_0'=4,'dom_1'=16,'dom_2'=2,'sub'=4] {'dom_2','sub'}, dimensions={0} | all-to-all | bytes 1052672 | tf_op jit(solution)/shard_map/all_to_all | solution.py:47
  86.4 17.5 %all_to_all.50 = f32[64,1,257]{2,1,0:T(1,128)S(1)} all-to-all(f32[64,1,257]{2,1,0:T(1,128)S(1)} %all_to_all.39), channel_id=1, replica_groups=mesh['dom_0'=4,'dom_1'=16,'dom_2'=2,'sub'=4] {'dom_0','dom_1'}, dimensions={0} | all-to-all | bytes 131584 | tf_op jit(solution)/shard_map/all_to_all | solution.py:54
  104.1 20.1 %all_to_all.51 = f32[64,1,257]{2,1,0:T(1,128)S(1)} all-to-all(f32[64,1,257]{2,1,0:T(1,128)S(1)} %broadcast_in_dim.13), channel_id=1, replica_groups=mesh['dom_0'=4,'dom_1'=16,'dom_2'=2,'sub'=4] {'dom_0','dom_1'}, dimensions={0} | all-to-all | bytes 131584 | tf_op jit(solution)/shard_map/all_to_all | solution.py:21
  124.2 0.9 broadcast_in_dim.30
  125.2 6.1 %all-to-all-start.5 = ((f32[8,64,257]{2,1,0:T(8,128)}), f32[8,64,257]{2,1,0:T(8,128)S(1)}, u32[]{:S(2)}, u32[]{:S(2)}) async-start(f32[8,64,257]{2,1,0:T(8,128)} %broadcast_in_dim.30), calls=%async_computation.5 | async-start | bytes 1572864 | tf_op jit(solution)/shard_map/all_to_all | solution.py:21
  131.3 12.1 %all-to-all-done.5 = f32[8,64,257]{2,1,0:T(8,128)S(1)} async-done(((f32[8,64,257]{2,1,0:T(8,128)}), f32[8,64,257]{2,1,0:T(8,128)S(1)}, u32[]{:S(2)}, u32[]{:S(2)}) %all-to-all-start.5) | async-done | bytes 526368 | tf_op jit(solution)/shard_map/all_to_all | solution.py:21
  143.9 0.8 slice.68
  144.8 0.8 fusion.27
  146.0 11.7 %cholesky.49 = f32[128,128]{1,0:T(8,128)S(1)} custom-call(f32[128,128]{1,0:T(8,128)S(1)} %cholesky.115), custom_call_target="Cholesky" | custom-call | tf_op jit(solution)/shard_map/jit(cholesky)/cholesky | solution.py:86
  157.8 9.8 %custom-call.14 = f32[1,128,128]{1,2,0:T(8,128)S(1)} custom-call(f32[1,128,128]{2,1,0:T(8,128)S(1)} %get-tuple-element.41), custom_call_target="InvertDiagBlocksLowerTriangular" | custom-call | tf_op jit(solution)/shard_map/jit(cholesky)/cholesky | solution.py:86
  168.2 11.7 %cholesky.103 = f32[128,128]{1,0:T(8,128)S(1)} custom-call(f32[128,128]{1,0:T(8,128)S(1)} %convolution_subtract_fusion.1), custom_call_target="Cholesky" | custom-call | tf_op jit(solution)/shard_map/jit(cholesky)/cholesky | solution.py:86
  182.7 4.2 %while.1 = (s32[]{:T(128)}, f32[256,256]{0,1:T(8,128)S(1)}, s32[2,2]{1,0:T(2,128)S(1)}, f32[2,128,128]{2,1,0:T(8,128)S(1)}, s32[]{:T(128)}) while((s32[]{:T(128)}, f32[256,256]{0,1:T(8,128)S(1)}, s32[2,2]{1,0:T(2,128)S(1)}, f32[2,128,128]{2,1,0:T(8,128)S(1)}, s32[]{:T(128)}) %tuple.32), condition=%wide.while_cond, body=%wide.while_body.sunk | while | flops 2 | bytes 393329 | solution.py:87
  183.4 1.3 dynamic-slice.7
  185.4 1.3 dynamic-slice.7
  186.9 19.7 %custom-call.15 = f32[2,128,128]{1,2,0:T(8,128)S(1)} custom-call(f32[2,128,128]{2,1,0:T(8,128)S(1)} %get-tuple-element.9), custom_call_target="InvertDiagBlocksLowerTriangular" | custom-call | tf_op jit(solution)/shard_map/triangular_solve | solution.py:87
  207.9 2.0 fusion.3
  209.8 1.4 reshape_reshape.7
  211.2 1.1 fusion
  212.4 1.1 copy.60
  214.1 1.3 slice.91
  (80 shorter events, 11.7 us)
Async XLA Ops:
  0.6 57.6 %copy-start = (bf16[16,128,128]{2,1,0:T(8,128)(2,1)S(1)}, bf16[16,128,128]{2,1,0:T(8,128)(2,1)}, u32[]{:S(2)}) copy-start(bf16[16,128,128]{2,1,0:T(8,128)(2,1)} %param.17) | copy-start | bytes 1572868
  0.6 24.7 %copy-start.1 = (bf16[1024,256]{1,0:T(8,128)(2,1)S(1)}, bf16[1024,256]{1,0:T(8,128)(2,1)}, u32[]{:S(2)}) copy-start(bf16[1024,256]{1,0:T(8,128)(2,1)} %param.9) | copy-start | bytes 1572868
  0.7 24.7 %copy-start.6 = (s32[128]{0:T(128)S(1)}, s32[128]{0:T(128)}, u32[]{:S(2)}) copy-start(s32[128]{0:T(128)} %param.12) | copy-start | bytes 1540
  0.7 26.2 %copy-start.7 = (s32[8]{0:T(128)S(1)}, s32[8]{0:T(128)}, u32[]{:S(2)}) copy-start(s32[8]{0:T(128)} %param.15) | copy-start | bytes 100
  0.7 26.2 %copy-start.8 = (s32[8]{0:T(128)S(1)}, s32[8]{0:T(128)}, u32[]{:S(2)}) copy-start(s32[8]{0:T(128)} %param.14) | copy-start | bytes 100
  0.7 26.2 %copy-start.3 = (s32[1,2]{1,0:T(1,128)S(1)}, s32[1,2]{1,0:T(1,128)}, u32[]{:S(2)}) copy-start(s32[1,2]{1,0:T(1,128)} %param.16) | copy-start | bytes 28
  4.9 42.9 %all-to-all-start = ((bf16[128,4,256]{2,1,0:T(4,128)(2,1)}), bf16[128,4,256]{2,1,0:T(4,128)(2,1)S(1)}, u32[]{:S(2)}, u32[]{:S(2)}) async-start(bf16[128,4,256]{2,1,0:T(4,128)(2,1)} %all_to_all.32), calls=%async_computation | async-start | bytes 524288 | tf_op jit(solution)/shard_map/all_to_all | solution.py:110
  47.8 8.7 %all-to-all-start.1 = ((bf16[4,32,256]{2,1,0:T(8,128)(2,1)}), bf16[4,32,256]{2,1,0:T(8,128)(2,1)S(1)}, u32[]{:S(2)}, u32[]{:S(2)}) async-start(bf16[4,32,256]{2,1,0:T(8,128)(2,1)} %bitcast.4), calls=%async_computation.1 | async-start | bytes 131072 | tf_op jit(solution)/shard_map/all_to_all | solution.py:111
  59.9 2.1 copy-start.4
  62.0 2.6 %copy-start.5 = (bf16[256,256]{1,0:T(8,128)(2,1)S(1)}, bf16[256,256]{1,0:T(8,128)(2,1)}, u32[]{:S(2)}) copy-start(bf16[256,256]{1,0:T(8,128)(2,1)} %param.10) | copy-start | bytes 393220
  125.2 18.3 %all-to-all-start.5 = ((f32[8,64,257]{2,1,0:T(8,128)}), f32[8,64,257]{2,1,0:T(8,128)S(1)}, u32[]{:S(2)}, u32[]{:S(2)}) async-start(f32[8,64,257]{2,1,0:T(8,128)} %broadcast_in_dim.30), calls=%async_computation.5 | async-start | bytes 1572864 | tf_op jit(solution)/shard_map/all_to_all | solution.py:21
  144.8 62.4 %copy-start.2 = (f32[514,256]{1,0:T(8,128)}, f32[514,256]{1,0:T(8,128)S(1)}, u32[]{:S(2)}) copy-start(f32[514,256]{1,0:T(8,128)S(1)} %slice.68) | copy-start | bytes 1579012
where the time goes:
time: 219 us; the launch traced here: 218 us
  other arithmetic  58.2 us (27%)
  blocking collectives  55.8 us (25%)
  waiting for transfers between devices  35.5 us (16%)
  starting transfers between devices  30.7 us (14%)
  local copies, waits for them, and re-layouts  22 us (10%)
  matrix products  10.8 us (5%)
  between operations  5.24 us (2%)
    another operation x7, other arithmetic, whiten_map(): lower = jnp.linalg.cholesky(scaled)  34.5 us
    all_to_all x1, starting transfers between devices, body(): lax.all_to_all(features[send_far], DOM, split_axis=0, concat_axis=0, tile...  20.4 us
    all_to_all x1, blocking collectives, sent_to_all(): lax.all_to_all(jnp.broadcast_to(value[None], (size, *value.shape)), axis,...  20.1 us
    another operation x3, other arithmetic, whiten_map(): lax.linalg.triangular_solve(lower, identity, left_side=True, lower=True)  19.7 us
    all_to_all x1, waiting for transfers between devices, body(): lax.all_to_all(features[send_far], DOM, split_axis=0, concat_axis=0, tile...  19 us
    all_to_all x1, blocking collectives, sum_at_owner(): pieces = lax.all_to_all(cut_along(value, dim, size), axis, 0, 0, tiled=True)  18.1 us
    all_to_all x1, blocking collectives, sum_by_axis(): return jnp.sum(lax.all_to_all(own, far, 0, 0, tiled=True), axis=0)  17.5 us
    all_to_all x1, waiting for transfers between devices, sent_to_all(): lax.all_to_all(jnp.broadcast_to(value[None], (size, *value.shape)), axis,...  12.1 us
  transfers between devices with their start and end apart: 3, of which 3 were waited for; matrix products, arithmetic and copies ran while one was open for 2% of the time, Pallas kernels for 0%

commit v1 on v0

v1 whole, which is shorter than its diff:
```python
import functools

import jax
import jax.numpy as jnp
from jax import lax
from jax.experimental import pallas as pl
from jax.experimental.pallas import tpu as pltpu
from jax.sharding import Mesh
from jax.sharding import PartitionSpec as P

MESH_AXES = ("x", "z", "c", "y")
DOM = ("x", "z", "c")

EPSILON = 1e-05
PANEL = 32
SUB = 8
LANES = 128

VMEM = pl.BlockSpec(memory_space=pltpu.VMEM)
SMEM = pl.BlockSpec(memory_space=pltpu.SMEM)


def iota(shape, dim):
    return lax.broadcasted_iota(jnp.int32, shape, dim)


def contract(a, b, dims, **kw):
    return lax.dot_general(a, b, (dims, ((), ())), preferred_element_type=jnp.float32, **kw)


def three_terms(x):
    high = x.astype(jnp.bfloat16)
    rest = x - high.astype(jnp.float32)
    middle = rest.astype(jnp.bfloat16)
    low = (rest - middle.astype(jnp.float32)).astype(jnp.bfloat16)
    return high, middle, low


def reciprocal_of(p):
    guess = pl.reciprocal(p, approx=True)
    guess = guess * (2.0 - p * guess)
    return guess * (2.0 - p * guess)


def eliminate_panel(rows, near, first_lane, width):
    groups = PANEL // SUB
    rows, near = list(rows), list(near)
    lane = iota((SUB, width), 1)
    sub = iota((SUB, width), 0)
    sub_lane = iota((SUB, LANES), 0)
    pivots = [None] * groups
    full = (SUB, LANES)
    for b in range(groups):
        start = first_lane + SUB * b
        in_block = (lane >= start) & (lane < start + SUB)
        unit = jnp.where(lane - start == sub, 1.0, 0.0)
        rows[b] = jnp.where(in_block, unit, rows[b])
        for g in range(b + 1, groups):
            rows[g] = jnp.where(in_block, 0.0, rows[g])
        column = [
            {g: jnp.broadcast_to(near[g][:, SUB * b + k : SUB * b + k + 1], full) for g in range(b, groups)}
            for k in range(SUB)
        ]
        entry = {
            (m, k): jnp.broadcast_to(column[k][b][m : m + 1, :], full) for k in range(SUB) for m in range(k, SUB)
        }
        pivot = jnp.ones(full, jnp.float32)
        for k in range(SUB):
            inverse = reciprocal_of(entry[k, k])
            pivot = jnp.where(sub_lane == k, entry[k, k], pivot)
            ratio = {m: entry[m, k] * inverse for m in range(k + 1, SUB)}
            for n in range(k + 1, SUB):
                for m in range(n, SUB):
                    entry[m, n] = entry[m, n] - ratio[m] * entry[n, k]
            scale = {g: column[k][g] * inverse for g in range(b, groups)}
            scale[b] = jnp.where(sub_lane > k, scale[b], 0.0)
            for m in range(k + 1, SUB):
                for g in range(b, groups):
                    column[m][g] = column[m][g] - scale[g] * entry[m, k]
            lead = jnp.broadcast_to(rows[b][k : k + 1, :], (SUB, width))
            lead_near = jnp.broadcast_to(near[b][k : k + 1, :], full)
            for g in range(b, groups):
                wide = jnp.concatenate([scale[g]] * (width // LANES), 1)
                rows[g] = rows[g] - wide * lead
            near[b] = near[b] - scale[b] * lead_near
            for g in range(b + 1, groups):
                near[g] = near[g] - scale[g] * lead_near
        pivots[b] = pivot
    return rows, pivots


def whiten_kernel(vertex_count, parts_ref, hidden_ref, white_ref, loss_ref, a_ref, v_ref):
    width = a_ref.shape[0]
    groups = PANEL // SUB
    left = parts_ref[:, 0:SUB, :].reshape(width, LANES)
    right = parts_ref[:, SUB : 2 * SUB, :].reshape(width, LANES)
    packed = jnp.concatenate([left, right], 1)
    row, col = iota((width, width), 0), iota((width, width), 1)
    gram = jnp.where(row >= col, packed, packed.T)
    a_ref[...] = gram / vertex_count + jnp.where(row == col, EPSILON, 0.0)

    def panel(j, carry):
        first = pl.multiple_of(j * PANEL, PANEL)
        block = a_ref[pl.ds(first, PANEL), :]
        turned = pltpu.roll(block, lax.rem(width - first, width), 1)[:, :LANES]
        rows, pivots = eliminate_panel(
            [block[SUB * g : SUB * g + SUB] for g in range(groups)],
            [turned[SUB * g : SUB * g + SUB] for g in range(groups)],
            first,
            width,
        )
        whole = jnp.concatenate(rows, 0)
        pivot = jnp.concatenate(pivots, 0)
        pivot = jnp.concatenate([pivot] * (width // LANES), 1)
        lane = iota((PANEL, width), 1)
        lower = lane <= iota((PANEL, width), 0) + first
        v_ref[pl.ds(first, PANEL), :] = jnp.where(lower, whole * lax.rsqrt(pivot), 0.0)
        h, m, l = three_terms(whole / pivot)
        hh, mm, ll = three_terms(jnp.where(lower | (lane >= first + PANEL), whole, 0.0))
        update = contract(
            jnp.concatenate([h, h, m, h, l, m], 0), jnp.concatenate([hh, mm, hh, ll, hh, mm], 0), ((0,), (0,))
        )
        lanes = iota((width, width), 1)
        kept = jnp.where((lanes >= first) & (lanes < first + PANEL), 0.0, a_ref[...])
        a_ref[...] = kept - update
        return carry

    lax.fori_loop(0, width // PANEL, panel, 0)

    inverse = v_ref[...]
    high = inverse.astype(jnp.bfloat16)
    low = (inverse - high.astype(jnp.float32)).astype(jnp.bfloat16)
    hidden = hidden_ref[...]
    white_ref[...] = (contract(hidden, high, ((1,), (1,))) + contract(hidden, low, ((1,), (1,)))).astype(white_ref.dtype)

    left = parts_ref[:, 0:SUB, :].reshape(width, LANES)
    right = parts_ref[:, SUB : 2 * SUB, :].reshape(width, LANES)
    packed = jnp.concatenate([left, right], 1)
    turned = packed.T
    gram = jnp.where(row >= col, packed, turned)
    cross = jnp.where(row > col, turned, 0.0)
    spare = parts_ref[:, 2 * SUB : 3 * SUB, :].reshape(width, LANES)
    square_sum = spare[0, LANES - 1]
    image = contract(inverse, gram, ((1,), (0,)), precision=lax.Precision.HIGHEST)
    half = row[:, :LANES] < LANES
    diagonal = jnp.where(half, inverse[:, :LANES], inverse[:, LANES:]) * spare
    doubled = inverse * (image - 2.0 * cross)
    total = jnp.sum(doubled) - 2.0 * jnp.sum(diagonal) + square_sum
    loss_ref[0, 0] = total / (vertex_count * width)


def whiten(parts, hidden, vertex_count):
    rows, width = hidden.shape
    return pl.pallas_call(
        functools.partial(whiten_kernel, vertex_count),
        out_shape=(jax.ShapeDtypeStruct((rows, width), jnp.bfloat16), jax.ShapeDtypeStruct((1, 1), jnp.float32)),
        in_specs=[VMEM, VMEM],
        out_specs=(VMEM, SMEM),
        scratch_shapes=[pltpu.VMEM((width, width), jnp.float32), pltpu.VMEM((width, width), jnp.float32)],
        compiler_params=pltpu.CompilerParams(vmem_limit_bytes=24 * 2**20),
    )(parts, hidden)


def pack(gram, cross, square_sum):
    width = gram.shape[0]
    row, col = iota((width, width), 0), iota((width, width), 1)
    both = jnp.where(row >= col, gram, cross)
    diagonal = jnp.where(row == col, cross, 0.0)
    half = row[:, :LANES] < LANES
    spare = jnp.where(half, diagonal[:, :LANES], diagonal[:, LANES:])
    corner = (row[:, :LANES] == 0) & (col[:, :LANES] == LANES - 1)
    spare = jnp.where(corner, square_sum, spare)
    shape = (width // SUB, SUB, LANES)
    return [both[:, :LANES].reshape(shape), both[:, LANES:].reshape(shape), spare.reshape(shape)]


def gather_kernel(features_ref, index_ref, out_ref):
    source = features_ref.shape[0]
    chunks = index_ref.shape[0]
    lane = iota((LANES, LANES), 1)
    features = features_ref[...]
    for r in range(chunks):
        wanted = jnp.broadcast_to(index_ref[r : r + 1, :].astype(jnp.float32), (LANES, LANES)).T.astype(jnp.int32)
        picks = [
            jnp.where(wanted == lane + LANES * s, 1.0, 0.0).astype(jnp.bfloat16) for s in range(source // LANES)
        ]
        picked = contract(jnp.concatenate(picks, 1), features, ((1,), (0,)))
        out_ref[LANES * r : LANES * r + LANES, :] = picked.astype(out_ref.dtype)


def gather(features, index):
    return pl.pallas_call(
        gather_kernel,
        out_shape=jax.ShapeDtypeStruct((index.size, features.shape[1]), features.dtype),
        in_specs=[VMEM, VMEM],
        out_specs=VMEM,
        compiler_params=pltpu.CompilerParams(vmem_limit_bytes=24 * 2**20),
    )(features, index.reshape(-1, LANES))


def layer_kernel(
    dst_ref, inner_ref, outer_ref, live_ref, features_ref, far_ref, near_ref, tile_ref, weight_ref,
    hidden_ref, parts_ref, sum_ref,
):
    slots, tile = inner_ref.shape[0], tile_ref.shape[1]
    far_tiles = far_ref.shape[0] // tile
    sum_ref[...] = jnp.zeros_like(sum_ref)

    def add(c, source):
        to = pl.ds(pl.multiple_of(dst_ref[c] * tile, tile), tile)
        sum_ref[to, :] += contract(tile_ref[c], source, ((1,), (0,)))

    def rows_of(ref, index):
        return ref[pl.ds(pl.multiple_of(index * tile, tile), tile), :]

    for k in range(slots):
        @pl.when(k < live_ref[0, 0])
        def _(k=k):
            add(k, rows_of(features_ref, inner_ref[k]))

        @pl.when((k < live_ref[0, 1]) & (outer_ref[k] < far_tiles))
        def _(k=k):
            add(slots + k, rows_of(far_ref, outer_ref[k]))

        @pl.when((k < live_ref[0, 1]) & (outer_ref[k] >= far_tiles))
        def _(k=k):
            add(slots + k, rows_of(near_ref, outer_ref[k] - far_tiles))

    projected = contract(sum_ref[...].astype(jnp.bfloat16), weight_ref[...], ((1,), (0,)))
    features = features_ref[...]
    wide = features.astype(jnp.float32)
    hidden = (wide + projected / (1.0 + jnp.exp(-projected))).astype(jnp.bfloat16)
    hidden_ref[...] = hidden
    gram = contract(hidden, hidden, ((0,), (0,)))
    cross = contract(hidden, features, ((0,), (0,)))
    for i, part in enumerate(pack(gram, cross, jnp.sum(wide * wide))):
        parts_ref[:, SUB * i : SUB * i + SUB, :] = part


def layer(dst, inner, outer, live, features, far, near, tiles, weight):
    rows, width = features.shape
    return pl.pallas_call(
        layer_kernel,
        out_shape=(
            jax.ShapeDtypeStruct((rows, width), jnp.bfloat16),
            jax.ShapeDtypeStruct((width // SUB, 3 * SUB, LANES), jnp.float32),
        ),
        in_specs=[SMEM] * 4 + [VMEM] * 5,
        out_specs=(VMEM, VMEM),
        scratch_shapes=[pltpu.VMEM((rows, width), jnp.float32)],
        compiler_params=pltpu.CompilerParams(vmem_limit_bytes=32 * 2**20),
    )(dst, inner, outer, live, features, far, near, tiles, weight)


def sum_over_all(parts):
    own = jnp.sum(lax.all_to_all(parts, ("x", "c", "y"), 0, 0, tiled=True), 0)
    z_size = lax.axis_size("z")
    own = jnp.broadcast_to(own[None], (z_size, *own.shape))
    own = jnp.sum(lax.all_to_all(own, "z", 0, 0, tiled=True), 0)
    own = jnp.broadcast_to(own[None], parts.shape)
    return lax.all_to_all(own, ("x", "c", "y"), 0, 0, tiled=True)


def body(
    features, weight, send_far, send_near, tile_dst, inner_src, outer_src, tile_live, tile_weight
):
    rows = features.shape[0]
    picked = gather(features, jnp.concatenate([send_far, send_near]))
    far_count = send_far.shape[0]
    far = picked[:far_count].reshape(lax.axis_size(DOM), -1, features.shape[1])
    far = lax.all_to_all(far, DOM, 0, 0, tiled=True).reshape(far_count, -1)
    near = lax.all_to_all(picked[far_count:], "y", 0, 0, tiled=True)
    hidden, parts = layer(
        tile_dst, inner_src, outer_src, tile_live, features, far, near, tile_weight, weight
    )
    parts = sum_over_all(parts)
    vertex_count = rows * lax.axis_size(DOM) * lax.axis_size("y")
    white, loss = whiten(parts, hidden, vertex_count)
    return white, loss[0, 0]


def solution(mesh):
    torus = Mesh(mesh.devices.reshape(4, 16, 2, mesh.shape["sub"]), MESH_AXES)
    whole = MESH_AXES
    return jax.shard_map(
        body,
        mesh=torus,
        in_specs=(
            P(whole, None), P(), P(whole), P(whole), P(whole), P(whole), P(whole), P(whole, None), P(whole, None, None),
        ),
        out_specs=(P(whole, None), P()),
        check_vma=False,
    )
```

time: 219 us -> 122 us (0.56)
  other arithmetic: 58.2 us -> 0.77 us
  local copies, waits for them, and re-layouts: 22 us -> 2.61 us
  Pallas kernels: 0 us -> 17 us
  matrix products: 10.8 us -> 0 us
  waiting for transfers between devices: 35.5 us -> 26.2 us
  blocking collectives: 55.8 us -> 49.4 us
  starting transfers between devices: 30.7 us -> 24.7 us
  between operations: 5.24 us -> 0.76 us
    another operation x10 -> x0, other arithmetic: 54.3 us -> none  [the longest x7 34.5 us: whiten_map(): lower = jnp.linalg.cholesky(scaled)]
    pallas_call x0 -> x3, Pallas kernels: none -> 17 us  [the longest x1 12.5 us: whiten(): pl.pallas_call(functools.partial(whiten_kernel, vertex_count), out_shape=...]
    dot_general x8 -> x0, matrix products: 9.36 us -> none  [the longest x1 2.44 us: aggregate_tiles(): jnp.einsum('tk,kif->tif', selector, products, precision=lax.Precision.HIG...]
    all_to_all x3 -> x2, waiting for transfers between devices: 35.5 us -> 26.2 us  [the longest x1 21.8 us: body(): far = lax.all_to_all(far, DOM, 0, 0, tiled=True).reshape(far_count, -1)]
    another operation x20 -> x0, local copies, waits for them, and re-layouts: 6.41 us -> none
    all_to_all x3, blocking collectives: 55.8 us -> 49.4 us  [the longest x1 17.2 us: sum_over_all(): return lax.all_to_all(own, ('x', 'c', 'y'), 0, 0, tiled=True)]
    all_to_all x3 -> x2, starting transfers between devices: 30.7 us -> 24.7 us  [the longest x1 20.5 us: body(): far = lax.all_to_all(far, DOM, 0, 0, tiled=True).reshape(far_count, -1)]
    gather x3 -> x0, local copies, waits for them, and re-layouts: 5.74 us -> none  [the longest x1 2.67 us: body(): features[send_far]]
  transfers between devices with their start and end apart: 3 -> 2, of which waited for: 3 -> 2; matrix products, arithmetic and copies ran while one was open for 2% -> 1% of each run, Pallas kernels for 0% -> 0%
where the time goes in v1:
time: 122 us; the launch traced here: 121 us
  blocking collectives  49.4 us (40%)
  waiting for transfers between devices  26.2 us (21%)
  starting transfers between devices  24.7 us (20%)
  Pallas kernels  17 us (14%)
  local copies, waits for them, and re-layouts  2.61 us (2%)
    all_to_all x1, waiting for transfers between devices, body(): far = lax.all_to_all(far, DOM, 0, 0, tiled=True).reshape(far_count, -1)  21.8 us
    all_to_all x1, starting transfers between devices, body(): far = lax.all_to_all(far, DOM, 0, 0, tiled=True).reshape(far_count, -1)  20.5 us
    all_to_all x1, blocking collectives, sum_over_all(): return lax.all_to_all(own, ('x', 'c', 'y'), 0, 0, tiled=True)  17.2 us
    all_to_all x1, blocking collectives, sum_over_all(): own = jnp.sum(lax.all_to_all(parts, ('x', 'c', 'y'), 0, 0, tiled=True), 0)  16.7 us
    all_to_all x1, blocking collectives, sum_over_all(): own = jnp.sum(lax.all_to_all(own, 'z', 0, 0, tiled=True), 0)  15.4 us
    pallas_call x1, Pallas kernels, whiten(): pl.pallas_call(functools.partial(whiten_kernel, vertex_count), out_shape=...  12.5 us
    all_to_all x1, waiting for transfers between devices, body(): near = lax.all_to_all(picked[far_count:], 'y', 0, 0, tiled=True)  4.37 us
    all_to_all x1, starting transfers between devices, body(): near = lax.all_to_all(picked[far_count:], 'y', 0, 0, tiled=True)  4.19 us
  transfers between devices with their start and end apart: 2, of which 2 were waited for; matrix products, arithmetic and copies ran while one was open for 1% of the time, Pallas kernels for 0%

profile of v1, /device:TPU:1, one launch (start us, length us, event | category | flops | bytes accessed | tf_op | source)
XLA Modules:
  0.0 121.5 jit_solution(2640213919809865727)
XLA Ops:
  0.6 0.7 add_bitcast_fusion.index_ref
  1.3 0.0 copy-start
  1.3 1.0 copy-done
  2.4 0.7 shard_map.104
  3.1 0.8 reshape.18
  3.8 0.0 copy-start.2
  3.8 20.5 %all-to-all-start = ((bf16[128,4,256]{2,1,0:T(4,128)(2,1)}), bf16[128,4,256]{2,1,0:T(4,128)(2,1)S(1)}, u32[]{:S(2)}, u32[]{:S(2)}) async-start(bf16[128,4,256]{2,1,0:T(4,128)(2,1)} %reshape.18), calls=%async_computation | async-start | bytes 524288 | tf_op jit(solution)/shard_map/all_to_all | solution.py:271
  24.4 0.0 copy-start.1
  24.4 0.6 slice.9
  25.0 21.8 %all-to-all-done = bf16[128,4,256]{2,1,0:T(4,128)(2,1)S(1)} async-done(((bf16[128,4,256]{2,1,0:T(4,128)(2,1)}), bf16[128,4,256]{2,1,0:T(4,128)(2,1)S(1)}, u32[]{:S(2)}, u32[]{:S(2)}) %all-to-all-start) | async-done | bytes 262176 | tf_op jit(solution)/shard_map/all_to_all | solution.py:271
  46.9 4.2 %all-to-all-start.1 = ((bf16[4,32,256]{2,1,0:T(8,128)(2,1)}), bf16[4,32,256]{2,1,0:T(8,128)(2,1)S(1)}, u32[]{:S(2)}, u32[]{:S(2)}) async-start(bf16[4,32,256]{2,1,0:T(8,128)(2,1)} %bitcast.1), calls=%async_computation.1 | async-start | bytes 131072 | tf_op jit(solution)/shard_map/all_to_all | solution.py:272
  51.1 0.0 copy-start.3
  51.1 0.0 copy-start.7
  51.1 0.1 reshape.19.far_ref
  51.1 0.0 copy-start.4
  51.1 0.0 copy-start.5
  51.2 0.0 copy-start.6
  51.2 4.4 %all-to-all-done.1 = bf16[4,32,256]{2,1,0:T(8,128)(2,1)S(1)} async-done(((bf16[4,32,256]{2,1,0:T(8,128)(2,1)}), bf16[4,32,256]{2,1,0:T(8,128)(2,1)S(1)}, u32[]{:S(2)}, u32[]{:S(2)}) %all-to-all-start.1) | async-done | bytes 65568 | tf_op jit(solution)/shard_map/all_to_all | solution.py:272
  55.5 0.0 copy-done.2
  55.5 0.0 copy-done.1
  55.5 0.0 copy-done.3
  55.5 0.0 copy-done.7
  55.6 0.0 copy-done.4
  55.6 0.0 copy-done.5
  55.6 0.0 copy-done.6
  55.6 3.9 %shard_map.105 = (bf16[1024,256]{1,0:T(8,128)(2,1)S(1)}, f32[32,24,128]{2,1,0:T(8,128)S(1)}) custom-call(s32[16]{0:T(128)S(1)} %copy-done.4, s32[8]{0:T(128)S(1)} %copy-done.5, s32[8]{0:T(128)S(1)} %copy-done.6, s32[1,2]{1,0:T(1,128)S(1)} %copy-done.7, bf16[1024,256]{1,0:T(8,128)(2,1)S(1)} %copy-done.1, bf16[512,256]{1,0:T(8,128)(2,1)S(1)} %reshape.19.far_ref, ...), custom_call_target="tpu_custom_call" | custom-call | tf_op jit(solution)/shard_map/pallas_call | solution.py:242
  59.5 16.7 %all_to_all.31 = f32[32,24,128]{2,1,0:T(8,128)S(1)} all-to-all(f32[32,24,128]{2,1,0:T(8,128)S(1)} %get-tuple-element.6), channel_id=1, replica_groups=mesh['x'=4,'z'=16,'c'=2,'y'=4] {'x','c','y'}, dimensions={0} | all-to-all | bytes 786432 | tf_op jit(solution)/shard_map/all_to_all | solution.py:256
  76.3 15.4 %all_to_all.32 = f32[16,24,128]{2,1,0:T(8,128)S(1)} all-to-all(f32[16,24,128]{2,1,0:T(8,128)S(1)} %broadcast_in_dim.4), channel_id=1, replica_groups=mesh['x'=4,'z'=16,'c'=2,'y'=4] {'z'}, dimensions={0} | all-to-all | bytes 393216 | tf_op jit(solution)/shard_map/all_to_all | solution.py:259
  91.8 17.2 %all_to_all.33.parts_ref = f32[32,24,128]{2,1,0:T(8,128)S(1)} all-to-all(f32[32,24,128]{2,1,0:T(8,128)S(1)} %broadcast_in_dim.5), channel_id=1, replica_groups=mesh['x'=4,'z'=16,'c'=2,'y'=4] {'x','c','y'}, dimensions={0} | all-to-all | bytes 786432 | tf_op jit(solution)/shard_map/all_to_all | solution.py:261
  109.0 12.5 %shard_map.106 = (bf16[1024,256]{1,0:T(8,128)(2,1)}, f32[1,1]{1,0:T(1,128)}) custom-call(f32[32,24,128]{2,1,0:T(8,128)S(1)} %all_to_all.33.parts_ref, bf16[1024,256]{1,0:T(8,128)(2,1)S(1)} %get-tuple-element.7.hidden_ref), custom_call_target="tpu_custom_call" | custom-call | tf_op jit(solution)/shard_map/pallas_call | solution.py:154
  (5 shorter events, 0.1 us)
Async XLA Ops:
  1.3 1.0 copy-start
  3.8 51.7 %copy-start.2 = (bf16[16,128,128]{2,1,0:T(8,128)(2,1)S(1)}, bf16[16,128,128]{2,1,0:T(8,128)(2,1)}, u32[]{:S(2)}) copy-start(bf16[16,128,128]{2,1,0:T(8,128)(2,1)} %tile_ref.1) | copy-start | bytes 1572868
  3.8 43.0 %all-to-all-start = ((bf16[128,4,256]{2,1,0:T(4,128)(2,1)}), bf16[128,4,256]{2,1,0:T(4,128)(2,1)S(1)}, u32[]{:S(2)}, u32[]{:S(2)}) async-start(bf16[128,4,256]{2,1,0:T(4,128)(2,1)} %reshape.18), calls=%async_computation | async-start | bytes 524288 | tf_op jit(solution)/shard_map/all_to_all | solution.py:271
  24.4 31.2 %copy-start.1 = (bf16[1024,256]{1,0:T(8,128)(2,1)S(1)}, bf16[1024,256]{1,0:T(8,128)(2,1)}, u32[]{:S(2)}) copy-start(bf16[1024,256]{1,0:T(8,128)(2,1)} %features_ref.3) | copy-start | bytes 1572868
  46.9 8.7 %all-to-all-start.1 = ((bf16[4,32,256]{2,1,0:T(8,128)(2,1)}), bf16[4,32,256]{2,1,0:T(8,128)(2,1)S(1)}, u32[]{:S(2)}, u32[]{:S(2)}) async-start(bf16[4,32,256]{2,1,0:T(8,128)(2,1)} %bitcast.1), calls=%async_computation.1 | async-start | bytes 131072 | tf_op jit(solution)/shard_map/all_to_all | solution.py:272
  51.1 4.5 %copy-start.3 = (bf16[256,256]{1,0:T(8,128)(2,1)S(1)}, bf16[256,256]{1,0:T(8,128)(2,1)}, u32[]{:S(2)}) copy-start(bf16[256,256]{1,0:T(8,128)(2,1)} %weight_ref.1) | copy-start | bytes 393220
  51.1 4.5 %copy-start.7 = (s32[1,2]{1,0:T(1,128)S(1)}, s32[1,2]{1,0:T(1,128)}, u32[]{:S(2)}) copy-start(s32[1,2]{1,0:T(1,128)} %live_ref.1) | copy-start | bytes 28
  51.1 4.4 %copy-start.4 = (s32[16]{0:T(128)S(1)}, s32[16]{0:T(128)}, u32[]{:S(2)}) copy-start(s32[16]{0:T(128)} %dst_ref.1) | copy-start | bytes 196
  51.1 4.4 %copy-start.5 = (s32[8]{0:T(128)S(1)}, s32[8]{0:T(128)}, u32[]{:S(2)}) copy-start(s32[8]{0:T(128)} %inner_ref.1) | copy-start | bytes 100
  51.2 4.4 %copy-start.6 = (s32[8]{0:T(128)S(1)}, s32[8]{0:T(128)}, u32[]{:S(2)}) copy-start(s32[8]{0:T(128)} %outer_ref.1) | copy-start | bytes 100

commit v2 on v1

--- a/solution.py
+++ b/solution.py
@@ -174,34 +174,56 @@
     return [both[:, :LANES].reshape(shape), both[:, LANES:].reshape(shape), spare.reshape(shape)]
 
 
-def gather_kernel(features_ref, index_ref, out_ref):
-    source = features_ref.shape[0]
-    chunks = index_ref.shape[0]
+def gather_kernel(place_ref, features_ref, far_index_ref, near_index_ref, far_ref, turned_ref, near_own_ref, *near_refs):
+    source, width = features_ref.shape
     lane = iota((LANES, LANES), 1)
     features = features_ref[...]
-    for r in range(chunks):
-        wanted = jnp.broadcast_to(index_ref[r : r + 1, :].astype(jnp.float32), (LANES, LANES)).T.astype(jnp.int32)
+
+    def rows_at(index):
+        wanted = jnp.broadcast_to(index.astype(jnp.float32), (LANES, LANES)).T.astype(jnp.int32)
         picks = [
             jnp.where(wanted == lane + LANES * s, 1.0, 0.0).astype(jnp.bfloat16) for s in range(source // LANES)
         ]
-        picked = contract(jnp.concatenate(picks, 1), features, ((1,), (0,)))
-        out_ref[LANES * r : LANES * r + LANES, :] = picked.astype(out_ref.dtype)
-
-
-def gather(features, index):
+        return contract(jnp.concatenate(picks, 1), features, ((1,), (0,)))
+
+    for r in range(far_index_ref.shape[0]):
+        picked = rows_at(far_index_ref[r : r + 1, :])
+        here = slice(LANES * r, LANES * r + LANES)
+        far_ref[here, :] = picked.astype(far_ref.dtype)
+        turned = pltpu.roll(picked.reshape(LANES // SUB, SUB, width), SUB // 2, 1)
+        turned_ref[here, :] = turned.reshape(LANES, width).astype(turned_ref.dtype)
+    picked = rows_at(near_index_ref[...]).astype(near_own_ref.dtype)
+    peers = 1 + len(near_refs)
+    block = LANES // peers
+    for k, ref in enumerate((near_own_ref, *near_refs)):
+        for q in range(peers):
+            @pl.when(lax.rem(place_ref[1] + k, peers) == q)
+            def _(ref=ref, q=q):
+                ref[...] = picked[block * q : block * q + block]
+
+
+def gather(place, features, far_index, near_index, peers):
+    width, dtype = features.shape[1], features.dtype
+    far = jax.ShapeDtypeStruct((far_index.size, width), dtype)
+    near = jax.ShapeDtypeStruct((near_index.size // peers, width), dtype)
     return pl.pallas_call(
         gather_kernel,
-        out_shape=jax.ShapeDtypeStruct((index.size, features.shape[1]), features.dtype),
-        in_specs=[VMEM, VMEM],
-        out_specs=VMEM,
+        out_shape=(far, far) + (near,) * peers,
+        in_specs=[SMEM, VMEM, VMEM, VMEM],
+        out_specs=(VMEM,) * (2 + peers),
         compiler_params=pltpu.CompilerParams(vmem_limit_bytes=24 * 2**20),
-    )(features, index.reshape(-1, LANES))
+    )(place, features, far_index.reshape(-1, LANES), near_index.reshape(-1, LANES))
 
 
 def layer_kernel(
-    dst_ref, inner_ref, outer_ref, live_ref, features_ref, far_ref, near_ref, tile_ref, weight_ref,
-    hidden_ref, parts_ref, sum_ref,
+    place_ref, dst_ref, inner_ref, outer_ref, live_ref, features_ref, far_ref, tile_ref, weight_ref, *rest
 ):
+    *near_refs, hidden_ref, parts_ref, sum_ref, near_ref = rest
+    peers = len(near_refs)
+    block = near_ref.shape[0] // peers
+    for k, ref in enumerate(near_refs):
+        at = lax.rem(place_ref[1] + peers - k, peers)
+        near_ref[pl.ds(pl.multiple_of(at * block, block), block), :] = ref[...]
     slots, tile = inner_ref.shape[0], tile_ref.shape[1]
     far_tiles = far_ref.shape[0] // tile
     sum_ref[...] = jnp.zeros_like(sum_ref)
@@ -237,19 +259,20 @@
         parts_ref[:, SUB * i : SUB * i + SUB, :] = part
 
 
-def layer(dst, inner, outer, live, features, far, near, tiles, weight):
+def layer(place, dst, inner, outer, live, features, far, tiles, weight, near):
     rows, width = features.shape
+    near_rows = sum(n.shape[0] for n in near)
     return pl.pallas_call(
         layer_kernel,
         out_shape=(
             jax.ShapeDtypeStruct((rows, width), jnp.bfloat16),
             jax.ShapeDtypeStruct((width // SUB, 3 * SUB, LANES), jnp.float32),
         ),
-        in_specs=[SMEM] * 4 + [VMEM] * 5,
+        in_specs=[SMEM] * 5 + [VMEM] * (4 + len(near)),
         out_specs=(VMEM, VMEM),
-        scratch_shapes=[pltpu.VMEM((rows, width), jnp.float32)],
+        scratch_shapes=[pltpu.VMEM((rows, width), jnp.float32), pltpu.VMEM((near_rows, width), features.dtype)],
         compiler_params=pltpu.CompilerParams(vmem_limit_bytes=32 * 2**20),
-    )(dst, inner, outer, live, features, far, near, tiles, weight)
+    )(place, dst, inner, outer, live, features, far, tiles, weight, *near)
 
 
 def sum_over_all(parts):
@@ -264,14 +287,20 @@
 def body(
     features, weight, send_far, send_near, tile_dst, inner_src, outer_src, tile_live, tile_weight
 ):
-    rows = features.shape[0]
-    picked = gather(features, jnp.concatenate([send_far, send_near]))
-    far_count = send_far.shape[0]
-    far = picked[:far_count].reshape(lax.axis_size(DOM), -1, features.shape[1])
-    far = lax.all_to_all(far, DOM, 0, 0, tiled=True).reshape(far_count, -1)
-    near = lax.all_to_all(picked[far_count:], "y", 0, 0, tiled=True)
+    rows, width = features.shape
+    core, y = lax.axis_index("c"), lax.axis_index("y")
+    peers = lax.axis_size("y")
+    place = jnp.stack([core, y]).astype(jnp.int32)
+    far, turned, *near = gather(place, features, send_far, send_near, peers)
+    crossed = lax.ppermute(turned, "c", [(0, 1), (1, 0)])
+    upper = iota((1, SUB, 1), 1) >= SUB // 2
+    mixed = jnp.where(upper == (core == 1), far.reshape(-1, SUB, width), crossed.reshape(-1, SUB, width))
+    far = lax.all_to_all(mixed, ("x", "z"), 0, 0, tiled=True).reshape(-1, width)
+    near = near[:1] + [
+        lax.ppermute(near[k], "y", [(i, (i + k) % peers) for i in range(peers)]) for k in range(1, peers)
+    ]
     hidden, parts = layer(
-        tile_dst, inner_src, outer_src, tile_live, features, far, near, tile_weight, weight
+        place, tile_dst, inner_src, outer_src, tile_live, features, far, tile_weight, weight, near
     )
     parts = sum_over_all(parts)
     vertex_count = rows * lax.axis_size(DOM) * lax.axis_size("y")

time: 122 us -> 117 us (0.959)
  waiting for transfers between devices: 26.2 us -> 10.2 us
  starting transfers between devices: 24.7 us -> 32.5 us
  blocking collectives: 49.4 us -> 52.7 us
    ppermute x0 -> x4, starting transfers between devices: none -> 19.5 us  [the longest x3 10.7 us: body(): lax.ppermute(near[k], 'y', [(i, (i + k) % peers) for i in range(peers)])]
    all_to_all x2 -> x1, waiting for transfers between devices: 26.2 us -> 7.27 us  [body(): far = lax.all_to_all(mixed, ('x', 'z'), 0, 0, tiled=True).reshape(-1, width)]
    all_to_all x2 -> x1, starting transfers between devices: 24.7 us -> 13 us  [body(): far = lax.all_to_all(mixed, ('x', 'z'), 0, 0, tiled=True).reshape(-1, width)]
    ppermute x0 -> x4, waiting for transfers between devices: none -> 2.9 us  [the longest x3 1.78 us: body(): lax.ppermute(near[k], 'y', [(i, (i + k) % peers) for i in range(peers)])]
    all_to_all x1, blocking collectives: 16.7 us -> 19 us  [sum_over_all(): own = jnp.sum(lax.all_to_all(parts, ('x', 'c', 'y'), 0, 0, tiled=True), 0)]
    unnamed x16 -> x20, local copies, waits for them, and re-layouts: 1.08 us -> 2.39 us
  transfers between devices with their start and end apart: 2 -> 5, of which waited for: 2 -> 3; matrix products, arithmetic and copies ran while one was open for 1% -> 0% of each run, Pallas kernels for 0% -> 0%
where the time goes in v2:
time: 117 us
  blocking collectives  52.7 us (45%)
  starting transfers between devices  32.5 us (28%)
  Pallas kernels  17.4 us (15%)
  waiting for transfers between devices  10.2 us (9%)
  local copies, waits for them, and re-layouts  2.43 us (2%)
    all_to_all x1, blocking collectives, sum_over_all(): own = jnp.sum(lax.all_to_all(parts, ('x', 'c', 'y'), 0, 0, tiled=True), 0)  19 us
    all_to_all x1, blocking collectives, sum_over_all(): return lax.all_to_all(own, ('x', 'c', 'y'), 0, 0, tiled=True)  18 us
    all_to_all x1, blocking collectives, sum_over_all(): own = jnp.sum(lax.all_to_all(own, 'z', 0, 0, tiled=True), 0)  15.8 us
    all_to_all x1, starting transfers between devices, body(): far = lax.all_to_all(mixed, ('x', 'z'), 0, 0, tiled=True).reshape(-1, width)  13 us
    pallas_call x1, Pallas kernels, whiten(): pl.pallas_call(functools.partial(whiten_kernel, vertex_count), out_shape=...  12.5 us
    ppermute x3, starting transfers between devices, body(): lax.ppermute(near[k], 'y', [(i, (i + k) % peers) for i in range(peers)])  10.7 us
    ppermute x1, starting transfers between devices, body(): crossed = lax.ppermute(turned, 'c', [(0, 1), (1, 0)])  8.78 us
    all_to_all x1, waiting for transfers between devices, body(): far = lax.all_to_all(mixed, ('x', 'z'), 0, 0, tiled=True).reshape(-1, width)  7.27 us
  transfers between devices with their start and end apart: 5, of which 3 were waited for; matrix products, arithmetic and copies ran while one was open for 0% of the time, Pallas kernels for 0%

profile of v2, /device:TPU:1, one launch (start us, length us, event | category | flops | bytes accessed | tf_op | source)
XLA Modules:
  0.0 117.0 jit_solution(12737242700719687518)
XLA Ops:
  0.6 0.1 pad_add_fusion.place_ref
  0.7 0.0 copy-start.4
  0.7 0.0 copy-start.9
  0.7 0.7 copy-done.4
  1.4 0.0 copy-done.9
  1.4 0.0 copy-start
  1.4 1.0 copy-done
  2.4 1.4 %shard_map.104 = (bf16[512,256]{1,0:T(8,128)(2,1)S(1)}, bf16[512,256]{1,0:T(8,128)(2,1)S(1)}, bf16[32,256]{1,0:T(8,128)(2,1)S(1)}, bf16[32,256]{1,0:T(8,128)(2,1...) custom-call(s32[2]{0:T(128)S(1)} %pad_add_fusion.place_ref, bf16[1024,256]{1,0:T(8,128)(2,1)S(1)} %copy-done, ...), custom_call_target="tpu_custom_call" | custom-call | tf_op jit(solution)/shard_map/pallas_call | solution.py:209
  3.8 8.8 %collective-permute-start = (bf16[512,256]{1,0:T(8,128)(2,1)S(1)}, bf16[512,256]{1,0:T(8,128)(2,1)S(1)}, u32[]{:S(2)}, u32[]{:S(2)}) collective-permute-start(bf16[512,256]{1,0:T(8,128)(2,1)S(1)} %get-tuple-element.13), channel_id=1, source_target_pairs={{0,4},{4,0},{1,5},{5,1},{2,6},{6,2},{3,7},{7,3},{8,12},{12,8},{9,1... | collective-permute-start | bytes 786440 | tf_op jit(solution)/shard_map/ppermute | solution.py:295
  12.6 1.1 collective-permute-done
  13.8 0.0 copy-start.1
  13.8 0.8 bitcast_select_fusion
  14.6 13.0 %all-to-all-start = ((bf16[64,8,256]{2,1,0:T(8,128)(2,1)}), bf16[64,8,256]{2,1,0:T(8,128)(2,1)S(1)}, u32[]{:S(2)}, u32[]{:S(2)}) async-start(bf16[64,8,256]{2,1,0:T(8,128)(2,1)} %bitcast_select_fusion), calls=%async_computation | async-start | bytes 524288 | tf_op jit(solution)/shard_map/all_to_all | solution.py:298
  27.6 3.2 %collective-permute-start.1 = (bf16[32,256]{1,0:T(8,128)(2,1)S(1)}, bf16[32,256]{1,0:T(8,128)(2,1)S(1)}, u32[]{:S(2)}, u32[]{:S(2)}) collective-permute-start(bf16[32,256]{1,0:T(8,128)(2,1)S(1)} %get-tuple-element.15), channel_id=1, source_target_pairs={{0,1},{1,2},{2,3},{3,0},{4,5},{5,6},{6,7},{7,4},{8,9},{9,10},{10,1... | collective-permute-start | bytes 49160 | tf_op jit(solution)/shard_map/ppermute | solution.py:300
  30.8 4.5 %collective-permute-start.2 = (bf16[32,256]{1,0:T(8,128)(2,1)S(1)}, bf16[32,256]{1,0:T(8,128)(2,1)S(1)}, u32[]{:S(2)}, u32[]{:S(2)}) collective-permute-start(bf16[32,256]{1,0:T(8,128)(2,1)S(1)} %get-tuple-element.16), channel_id=1, source_target_pairs={{0,2},{1,3},{2,0},{3,1},{4,6},{5,7},{6,4},{7,5},{8,10},{9,11},{10,... | collective-permute-start | bytes 49160 | tf_op jit(solution)/shard_map/ppermute | solution.py:300
  35.4 3.0 %collective-permute-start.3 = (bf16[32,256]{1,0:T(8,128)(2,1)S(1)}, bf16[32,256]{1,0:T(8,128)(2,1)S(1)}, u32[]{:S(2)}, u32[]{:S(2)}) collective-permute-start(bf16[32,256]{1,0:T(8,128)(2,1)S(1)} %get-tuple-element.17), channel_id=1, source_target_pairs={{0,3},{1,0},{2,1},{3,2},{4,7},{5,4},{6,5},{7,6},{8,11},{9,8},{10,9... | collective-permute-start | bytes 49160 | tf_op jit(solution)/shard_map/ppermute | solution.py:300
  38.3 0.0 collective-permute-done.1.rest_1_
  38.3 0.0 collective-permute-done.2.rest_2_
  38.4 1.8 %collective-permute-done.3.rest_3_ = bf16[32,256]{1,0:T(8,128)(2,1)S(1)} collective-permute-done((bf16[32,256]{1,0:T(8,128)(2,1)S(1)}, bf16[32,256]{1,0:T(8,128)(2,1)S(1)}, u32[]{:S(2)}, u32[]{:S(2)}) %collective-permute-start.3) | collective-permute-done | bytes 16416 | tf_op jit(solution)/shard_map/ppermute | solution.py:300
  40.1 7.3 %all-to-all-done = bf16[64,8,256]{2,1,0:T(8,128)(2,1)S(1)} async-done(((bf16[64,8,256]{2,1,0:T(8,128)(2,1)}), bf16[64,8,256]{2,1,0:T(8,128)(2,1)S(1)}, u32[]{:S(2)}, u32[]{:S(2)}) %all-to-all-start) | async-done | bytes 262176 | tf_op jit(solution)/shard_map/all_to_all | solution.py:298
  47.4 0.0 copy-done.1
  47.4 0.0 copy-done.2
  47.4 0.0 copy-done.3
  47.4 0.0 copy-done.8
  47.4 0.6 copy-done.5
  48.1 0.0 copy-done.6
  48.1 0.0 copy-done.7
  48.1 3.5 %shard_map.105 = (bf16[1024,256]{1,0:T(8,128)(2,1)S(1)}, f32[32,24,128]{2,1,0:T(8,128)S(1)}) custom-call(s32[2]{0:T(128)S(1)} %pad_add_fusion.place_ref, s32[16]{0:T(128)S(1)} %copy-done.5, s32[8]{0:T(128)S(1)} %copy-done.6, s32[8]{0:T(128)S(1)} %copy-done.7, s32[1,2]{1,0:T(1,128)S(1)} %copy-done.8, bf16[1024,256]{1,0:T(8,128)(2,1)S(1)} %copy-done.1, ...), custom_call_target="tpu_custom_call" | custom-call | tf_op jit(solution)/shard_map/pallas_call | solution.py:265
  51.6 19.0 %all_to_all.20 = f32[32,24,128]{2,1,0:T(8,128)S(1)} all-to-all(f32[32,24,128]{2,1,0:T(8,128)S(1)} %get-tuple-element.18), channel_id=1, replica_groups=mesh['x'=4,'z'=16,'c'=2,'y'=4] {'x','c','y'}, dimensions={0} | all-to-all | bytes 786432 | tf_op jit(solution)/shard_map/all_to_all | solution.py:279
  70.7 15.8 %all_to_all.21 = f32[16,24,128]{2,1,0:T(8,128)S(1)} all-to-all(f32[16,24,128]{2,1,0:T(8,128)S(1)} %broadcast_in_dim.13), channel_id=1, replica_groups=mesh['x'=4,'z'=16,'c'=2,'y'=4] {'z'}, dimensions={0} | all-to-all | bytes 393216 | tf_op jit(solution)/shard_map/all_to_all | solution.py:282
  86.5 18.0 %all_to_all.22.parts_ref = f32[32,24,128]{2,1,0:T(8,128)S(1)} all-to-all(f32[32,24,128]{2,1,0:T(8,128)S(1)} %broadcast_in_dim.22), channel_id=1, replica_groups=mesh['x'=4,'z'=16,'c'=2,'y'=4] {'x','c','y'}, dimensions={0} | all-to-all | bytes 786432 | tf_op jit(solution)/shard_map/all_to_all | solution.py:284
  104.5 12.5 %shard_map.106 = (bf16[1024,256]{1,0:T(8,128)(2,1)}, f32[1,1]{1,0:T(1,128)}) custom-call(f32[32,24,128]{2,1,0:T(8,128)S(1)} %all_to_all.22.parts_ref, bf16[1024,256]{1,0:T(8,128)(2,1)S(1)} %get-tuple-element.19.hidden_ref), custom_call_target="tpu_custom_call" | custom-call | tf_op jit(solution)/shard_map/pallas_call | solution.py:154
  (11 shorter events, 0.1 us)
Async XLA Ops:
  0.7 0.7 copy-start.4
  0.7 0.7 copy-start.9
  1.4 1.0 copy-start
  3.8 9.9 %collective-permute-start = (bf16[512,256]{1,0:T(8,128)(2,1)S(1)}, bf16[512,256]{1,0:T(8,128)(2,1)S(1)}, u32[]{:S(2)}, u32[]{:S(2)}) collective-permute-start(bf16[512,256]{1,0:T(8,128)(2,1)S(1)} %get-tuple-element.13), channel_id=1, source_target_pairs={{0,4},{4,0},{1,5},{5,1},{2,6},{6,2},{3,7},{7,3},{8,12},{12,8},{9,1... | collective-permute-start | bytes 786440 | tf_op jit(solution)/shard_map/ppermute | solution.py:295
  13.8 33.7 %copy-start.1 = (bf16[1024,256]{1,0:T(8,128)(2,1)S(1)}, bf16[1024,256]{1,0:T(8,128)(2,1)}, u32[]{:S(2)}) copy-start(bf16[1024,256]{1,0:T(8,128)(2,1)} %features_ref.3) | copy-start | bytes 1572868
  13.8 33.7 %copy-start.2 = (bf16[16,128,128]{2,1,0:T(8,128)(2,1)S(1)}, bf16[16,128,128]{2,1,0:T(8,128)(2,1)}, u32[]{:S(2)}) copy-start(bf16[16,128,128]{2,1,0:T(8,128)(2,1)} %tile_ref.1) | copy-start | bytes 1572868
  14.6 32.9 %copy-start.3 = (bf16[256,256]{1,0:T(8,128)(2,1)S(1)}, bf16[256,256]{1,0:T(8,128)(2,1)}, u32[]{:S(2)}) copy-start(bf16[256,256]{1,0:T(8,128)(2,1)} %weight_ref.1) | copy-start | bytes 393220
  14.6 32.9 %copy-start.8 = (s32[1,2]{1,0:T(1,128)S(1)}, s32[1,2]{1,0:T(1,128)}, u32[]{:S(2)}) copy-start(s32[1,2]{1,0:T(1,128)} %live_ref.1) | copy-start | bytes 28
  14.6 32.8 %all-to-all-start = ((bf16[64,8,256]{2,1,0:T(8,128)(2,1)}), bf16[64,8,256]{2,1,0:T(8,128)(2,1)S(1)}, u32[]{:S(2)}, u32[]{:S(2)}) async-start(bf16[64,8,256]{2,1,0:T(8,128)(2,1)} %bitcast_select_fusion), calls=%async_computation | async-start | bytes 524288 | tf_op jit(solution)/shard_map/all_to_all | solution.py:298
  27.6 10.7 %collective-permute-start.1 = (bf16[32,256]{1,0:T(8,128)(2,1)S(1)}, bf16[32,256]{1,0:T(8,128)(2,1)S(1)}, u32[]{:S(2)}, u32[]{:S(2)}) collective-permute-start(bf16[32,256]{1,0:T(8,128)(2,1)S(1)} %get-tuple-element.15), channel_id=1, source_target_pairs={{0,1},{1,2},{2,3},{3,0},{4,5},{5,6},{6,7},{7,4},{8,9},{9,10},{10,1... | collective-permute-start | bytes 49160 | tf_op jit(solution)/shard_map/ppermute | solution.py:300
  30.8 7.5 %collective-permute-start.2 = (bf16[32,256]{1,0:T(8,128)(2,1)S(1)}, bf16[32,256]{1,0:T(8,128)(2,1)S(1)}, u32[]{:S(2)}, u32[]{:S(2)}) collective-permute-start(bf16[32,256]{1,0:T(8,128)(2,1)S(1)} %get-tuple-element.16), channel_id=1, source_target_pairs={{0,2},{1,3},{2,0},{3,1},{4,6},{5,7},{6,4},{7,5},{8,10},{9,11},{10,... | collective-permute-start | bytes 49160 | tf_op jit(solution)/shard_map/ppermute | solution.py:300
  35.4 4.8 %collective-permute-start.3 = (bf16[32,256]{1,0:T(8,128)(2,1)S(1)}, bf16[32,256]{1,0:T(8,128)(2,1)S(1)}, u32[]{:S(2)}, u32[]{:S(2)}) collective-permute-start(bf16[32,256]{1,0:T(8,128)(2,1)S(1)} %get-tuple-element.17), channel_id=1, source_target_pairs={{0,3},{1,0},{2,1},{3,2},{4,7},{5,4},{6,5},{7,6},{8,11},{9,8},{10,9... | collective-permute-start | bytes 49160 | tf_op jit(solution)/shard_map/ppermute | solution.py:300
  47.4 0.7 copy-start.5
  47.4 0.7 copy-start.6
  47.4 0.7 copy-start.7

commit v3 on v2

--- a/solution.py
+++ b/solution.py
@@ -34,12 +34,6 @@
     middle = rest.astype(jnp.bfloat16)
     low = (rest - middle.astype(jnp.float32)).astype(jnp.bfloat16)
     return high, middle, low
-
-
-def reciprocal_of(p):
-    guess = pl.reciprocal(p, approx=True)
-    guess = guess * (2.0 - p * guess)
-    return guess * (2.0 - p * guess)
 
 
 def eliminate_panel(rows, near, first_lane, width):
@@ -58,33 +52,51 @@
         for g in range(b + 1, groups):
             rows[g] = jnp.where(in_block, 0.0, rows[g])
         column = [
-            {g: jnp.broadcast_to(near[g][:, SUB * b + k : SUB * b + k + 1], full) for g in range(b, groups)}
+            {g: jnp.take_along_axis(near[g], jnp.full(full, SUB * b + k, jnp.int32), 1, mode='promise_in_bounds') for g in range(b, groups)}
             for k in range(SUB)
         ]
         entry = {
             (m, k): jnp.broadcast_to(column[k][b][m : m + 1, :], full) for k in range(SUB) for m in range(k, SUB)
         }
         pivot = jnp.ones(full, jnp.float32)
-        for k in range(SUB):
-            inverse = reciprocal_of(entry[k, k])
-            pivot = jnp.where(sub_lane == k, entry[k, k], pivot)
-            ratio = {m: entry[m, k] * inverse for m in range(k + 1, SUB)}
-            for n in range(k + 1, SUB):
+        for k in range(0, SUB, 2):
+            p, side, q = entry[k, k], entry[k + 1, k], entry[k + 1, k + 1]
+            det = p * q - side * side
+            inverse = pl.reciprocal(p)
+            both = pl.reciprocal(p * det)
+            second = both * p
+            pivot = jnp.where(sub_lane == k, p, jnp.where(sub_lane == k + 1, det * inverse, pivot))
+            left = {m: entry[m, k] for m in range(k + 2, SUB)}
+            right = {m: p * entry[m, k + 1] - side * entry[m, k] for m in range(k + 2, SUB)}
+            for n in range(k + 2, SUB):
                 for m in range(n, SUB):
-                    entry[m, n] = entry[m, n] - ratio[m] * entry[n, k]
-            scale = {g: column[k][g] * inverse for g in range(b, groups)}
-            scale[b] = jnp.where(sub_lane > k, scale[b], 0.0)
-            for m in range(k + 1, SUB):
+                    entry[m, n] = (entry[m, n] - left[m] * left[n] * inverse) - right[m] * right[n] * both
+            first_scale, second_scale = {}, {}
+            for g in range(b, groups):
+                x, y = column[k][g], column[k + 1][g]
+                first_scale[g] = x * inverse
+                second_scale[g] = (p * y - side * x) * second
+            first_scale[b] = jnp.where(sub_lane > k, first_scale[b], 0.0)
+            second_scale[b] = jnp.where(sub_lane > k + 1, second_scale[b], 0.0)
+            for m in range(k + 2, SUB):
+                reduced = right[m] * inverse
                 for g in range(b, groups):
-                    column[m][g] = column[m][g] - scale[g] * entry[m, k]
-            lead = jnp.broadcast_to(rows[b][k : k + 1, :], (SUB, width))
-            lead_near = jnp.broadcast_to(near[b][k : k + 1, :], full)
+                    column[m][g] = column[m][g] - first_scale[g] * left[m] - second_scale[g] * reduced
+            ratio = side * inverse
+
+            def lead_of(x):
+                shape = (SUB, x.shape[1])
+                first = jnp.broadcast_to(x[k : k + 1, :], shape)
+                wide = jnp.concatenate([ratio] * (x.shape[1] // LANES), 1)
+                return first, jnp.broadcast_to(x[k + 1 : k + 2, :], shape) - wide * first
+
+            lead = lead_of(rows[b])
+            lead_near = lead_of(near[b])
             for g in range(b, groups):
-                wide = jnp.concatenate([scale[g]] * (width // LANES), 1)
-                rows[g] = rows[g] - wide * lead
-            near[b] = near[b] - scale[b] * lead_near
-            for g in range(b + 1, groups):
-                near[g] = near[g] - scale[g] * lead_near
+                one = jnp.concatenate([first_scale[g]] * (width // LANES), 1)
+                two = jnp.concatenate([second_scale[g]] * (width // LANES), 1)
+                rows[g] = rows[g] - one * lead[0] - two * lead[1]
+                near[g] = near[g] - first_scale[g] * lead_near[0] - second_scale[g] * lead_near[1]
         pivots[b] = pivot
     return rows, pivots
 
@@ -92,9 +104,7 @@
 def whiten_kernel(vertex_count, parts_ref, hidden_ref, white_ref, loss_ref, a_ref, v_ref):
     width = a_ref.shape[0]
     groups = PANEL // SUB
-    left = parts_ref[:, 0:SUB, :].reshape(width, LANES)
-    right = parts_ref[:, SUB : 2 * SUB, :].reshape(width, LANES)
-    packed = jnp.concatenate([left, right], 1)
+    packed = jnp.concatenate([parts_ref[:width, :], parts_ref[width : 2 * width, :]], 1)
     row, col = iota((width, width), 0), iota((width, width), 1)
     gram = jnp.where(row >= col, packed, packed.T)
     a_ref[...] = gram / vertex_count + jnp.where(row == col, EPSILON, 0.0)
@@ -125,7 +135,7 @@
         a_ref[...] = kept - update
         return carry
 
-    lax.fori_loop(0, width // PANEL, panel, 0)
+    lax.fori_loop(0, width // PANEL, panel, 0, unroll=True)
 
     inverse = v_ref[...]
     high = inverse.astype(jnp.bfloat16)
@@ -133,17 +143,14 @@
     hidden = hidden_ref[...]
     white_ref[...] = (contract(hidden, high, ((1,), (1,))) + contract(hidden, low, ((1,), (1,)))).astype(white_ref.dtype)
 
-    left = parts_ref[:, 0:SUB, :].reshape(width, LANES)
-    right = parts_ref[:, SUB : 2 * SUB, :].reshape(width, LANES)
-    packed = jnp.concatenate([left, right], 1)
+    packed = jnp.concatenate([parts_ref[:width, :], parts_ref[width : 2 * width, :]], 1)
     turned = packed.T
     gram = jnp.where(row >= col, packed, turned)
     cross = jnp.where(row > col, turned, 0.0)
-    spare = parts_ref[:, 2 * SUB : 3 * SUB, :].reshape(width, LANES)
+    spare = parts_ref[2 * width :, :]
     square_sum = spare[0, LANES - 1]
     image = contract(inverse, gram, ((1,), (0,)), precision=lax.Precision.HIGHEST)
-    half = row[:, :LANES] < LANES
-    diagonal = jnp.where(half, inverse[:, :LANES], inverse[:, LANES:]) * spare
+    diagonal = diagonal_of(inverse) * spare
     doubled = inverse * (image - 2.0 * cross)
     total = jnp.sum(doubled) - 2.0 * jnp.sum(diagonal) + square_sum
     loss_ref[0, 0] = total / (vertex_count * width)
@@ -161,17 +168,21 @@
     )(parts, hidden)
 
 
+def diagonal_of(square):
+    width = square.shape[0]
+    row, col = iota((width, width), 0), iota((width, width), 1)
+    kept = jnp.where(row == col, square, 0.0)
+    kept = jnp.where(row[:, :LANES] < LANES, kept[:, :LANES], kept[:, LANES:])
+    return jnp.sum(kept.reshape(width // SUB, SUB, LANES), 1)
+
+
 def pack(gram, cross, square_sum):
     width = gram.shape[0]
     row, col = iota((width, width), 0), iota((width, width), 1)
     both = jnp.where(row >= col, gram, cross)
-    diagonal = jnp.where(row == col, cross, 0.0)
-    half = row[:, :LANES] < LANES
-    spare = jnp.where(half, diagonal[:, :LANES], diagonal[:, LANES:])
-    corner = (row[:, :LANES] == 0) & (col[:, :LANES] == LANES - 1)
-    spare = jnp.where(corner, square_sum, spare)
-    shape = (width // SUB, SUB, LANES)
-    return [both[:, :LANES].reshape(shape), both[:, LANES:].reshape(shape), spare.reshape(shape)]
+    spare = diagonal_of(cross)
+    corner = (iota(spare.shape, 0) == 0) & (iota(spare.shape, 1) == LANES - 1)
+    return [both[:, :LANES], both[:, LANES:], jnp.where(corner, square_sum, spare)]
 
 
 def gather_kernel(place_ref, features_ref, far_index_ref, near_index_ref, far_ref, turned_ref, near_own_ref, *near_refs):
@@ -255,8 +266,10 @@
     hidden_ref[...] = hidden
     gram = contract(hidden, hidden, ((0,), (0,)))
     cross = contract(hidden, features, ((0,), (0,)))
-    for i, part in enumerate(pack(gram, cross, jnp.sum(wide * wide))):
-        parts_ref[:, SUB * i : SUB * i + SUB, :] = part
+    first = 0
+    for part in pack(gram, cross, jnp.sum(wide * wide)):
+        parts_ref[first : first + part.shape[0], :] = part
+        first += part.shape[0]
 
 
 def layer(place, dst, inner, outer, live, features, far, tiles, weight, near):
@@ -266,7 +279,7 @@
         layer_kernel,
         out_shape=(
             jax.ShapeDtypeStruct((rows, width), jnp.bfloat16),
-            jax.ShapeDtypeStruct((width // SUB, 3 * SUB, LANES), jnp.float32),
+            jax.ShapeDtypeStruct((2 * width + width // SUB, LANES), jnp.float32),
         ),
         in_specs=[SMEM] * 5 + [VMEM] * (4 + len(near)),
         out_specs=(VMEM, VMEM),
@@ -276,12 +289,13 @@
 
 
 def sum_over_all(parts):
-    own = jnp.sum(lax.all_to_all(parts, ("x", "c", "y"), 0, 0, tiled=True), 0)
-    z_size = lax.axis_size("z")
-    own = jnp.broadcast_to(own[None], (z_size, *own.shape))
-    own = jnp.sum(lax.all_to_all(own, "z", 0, 0, tiled=True), 0)
-    own = jnp.broadcast_to(own[None], parts.shape)
-    return lax.all_to_all(own, ("x", "c", "y"), 0, 0, tiled=True)
+    near, far = ("x", "c", "y"), "z"
+    pieces = parts.reshape(lax.axis_size(near), 1, -1)
+    own = jnp.sum(lax.all_to_all(pieces, near, 0, 0, tiled=True), 0)
+    own = jnp.broadcast_to(own[None], (lax.axis_size(far), *own.shape))
+    own = jnp.sum(lax.all_to_all(own, far, 0, 0, tiled=True), 0)
+    own = jnp.broadcast_to(own[None], pieces.shape)
+    return lax.all_to_all(own, near, 0, 0, tiled=True).reshape(parts.shape)
 
 
 def body(

time: 117 us -> 110 us (0.940)
  Pallas kernels: 17.4 us -> 13.3 us
  blocking collectives: 52.7 us -> 49 us
    pallas_call x1, Pallas kernels: 12.5 us -> 8.28 us  [whiten(): pl.pallas_call(functools.partial(whiten_kernel, vertex_count), out_shape=...]
    all_to_all x3, blocking collectives: 52.7 us -> 49 us  [the longest x1 17.9 us: sum_over_all(): own = jnp.sum(lax.all_to_all(pieces, near, 0, 0, tiled=True), 0)]
where the time goes in v3:
time: 110 us
  blocking collectives  49 us (45%)
  starting transfers between devices  32.5 us (30%)
  Pallas kernels  13.3 us (12%)
  waiting for transfers between devices  10.2 us (9%)
  local copies, waits for them, and re-layouts  2.61 us (2%)
  other arithmetic  1.14 us (1%)
    all_to_all x1, blocking collectives, sum_over_all(): own = jnp.sum(lax.all_to_all(pieces, near, 0, 0, tiled=True), 0)  17.9 us
    all_to_all x1, blocking collectives, sum_over_all(): return lax.all_to_all(own, near, 0, 0, tiled=True).reshape(parts.shape)  15.8 us
    all_to_all x1, blocking collectives, sum_over_all(): own = jnp.sum(lax.all_to_all(own, far, 0, 0, tiled=True), 0)  15.2 us
    all_to_all x1, starting transfers between devices, body(): far = lax.all_to_all(mixed, ('x', 'z'), 0, 0, tiled=True).reshape(-1, width)  13 us
    ppermute x3, starting transfers between devices, body(): lax.ppermute(near[k], 'y', [(i, (i + k) % peers) for i in range(peers)])  10.7 us
    ppermute x1, starting transfers between devices, body(): crossed = lax.ppermute(turned, 'c', [(0, 1), (1, 0)])  8.78 us
    pallas_call x1, Pallas kernels, whiten(): pl.pallas_call(functools.partial(whiten_kernel, vertex_count), out_shape=...  8.28 us
    all_to_all x1, waiting for transfers between devices, body(): far = lax.all_to_all(mixed, ('x', 'z'), 0, 0, tiled=True).reshape(-1, width)  7.27 us
  transfers between devices with their start and end apart: 5, of which 3 were waited for; matrix products, arithmetic and copies ran while one was open for 0% of the time, Pallas kernels for 0%

profile of v3, /device:TPU:1, one launch (start us, length us, event | category | flops | bytes accessed | tf_op | source)
XLA Modules:
  0.0 109.5 jit_solution(1346685775119974595)
XLA Ops:
  0.6 0.1 pad_add_fusion.place_ref
  0.7 0.7 copy-done.4
  1.4 0.0 copy-done.9
  1.4 1.0 copy-done
  2.4 1.4 %shard_map.104 = (bf16[512,256]{1,0:T(8,128)(2,1)S(1)}, bf16[512,256]{1,0:T(8,128)(2,1)S(1)}, bf16[32,256]{1,0:T(8,128)(2,1)S(1)}, bf16[32,256]{1,0:T(8,128)(2,1...) custom-call(s32[2]{0:T(128)S(1)} %pad_add_fusion.place_ref, bf16[1024,256]{1,0:T(8,128)(2,1)S(1)} %copy-done, ...), custom_call_target="tpu_custom_call" | custom-call | tf_op jit(solution)/shard_map/pallas_call | solution.py:220
  3.8 8.8 %collective-permute-start = (bf16[512,256]{1,0:T(8,128)(2,1)S(1)}, bf16[512,256]{1,0:T(8,128)(2,1)S(1)}, u32[]{:S(2)}, u32[]{:S(2)}) collective-permute-start(bf16[512,256]{1,0:T(8,128)(2,1)S(1)} %get-tuple-element.13), channel_id=1, source_target_pairs={{0,4},{4,0},{1,5},{5,1},{2,6},{6,2},{3,7},{7,3},{8,12},{12,8},{9,1... | collective-permute-start | bytes 786440 | tf_op jit(solution)/shard_map/ppermute | solution.py:309
  12.6 1.1 %collective-permute-done = bf16[512,256]{1,0:T(8,128)(2,1)S(1)} collective-permute-done((bf16[512,256]{1,0:T(8,128)(2,1)S(1)}, bf16[512,256]{1,0:T(8,128)(2,1)S(1)}, u32[]{:S(2)}, u32[]{:S(2)}) %collective-permute-start) | collective-permute-done | bytes 262176 | tf_op jit(solution)/shard_map/ppermute | solution.py:309
  13.8 0.8 bitcast_select_fusion
  14.6 13.0 %all-to-all-start = ((bf16[64,8,256]{2,1,0:T(8,128)(2,1)}), bf16[64,8,256]{2,1,0:T(8,128)(2,1)S(1)}, u32[]{:S(2)}, u32[]{:S(2)}) async-start(bf16[64,8,256]{2,1,0:T(8,128)(2,1)} %bitcast_select_fusion), calls=%async_computation | async-start | bytes 524288 | tf_op jit(solution)/shard_map/all_to_all | solution.py:312
  27.6 3.2 %collective-permute-start.1 = (bf16[32,256]{1,0:T(8,128)(2,1)S(1)}, bf16[32,256]{1,0:T(8,128)(2,1)S(1)}, u32[]{:S(2)}, u32[]{:S(2)}) collective-permute-start(bf16[32,256]{1,0:T(8,128)(2,1)S(1)} %get-tuple-element.15), channel_id=1, source_target_pairs={{0,1},{1,2},{2,3},{3,0},{4,5},{5,6},{6,7},{7,4},{8,9},{9,10},{10,1... | collective-permute-start | bytes 49160 | tf_op jit(solution)/shard_map/ppermute | solution.py:314
  30.8 4.5 %collective-permute-start.2 = (bf16[32,256]{1,0:T(8,128)(2,1)S(1)}, bf16[32,256]{1,0:T(8,128)(2,1)S(1)}, u32[]{:S(2)}, u32[]{:S(2)}) collective-permute-start(bf16[32,256]{1,0:T(8,128)(2,1)S(1)} %get-tuple-element.16), channel_id=1, source_target_pairs={{0,2},{1,3},{2,0},{3,1},{4,6},{5,7},{6,4},{7,5},{8,10},{9,11},{10,... | collective-permute-start | bytes 49160 | tf_op jit(solution)/shard_map/ppermute | solution.py:314
  35.4 3.0 %collective-permute-start.3 = (bf16[32,256]{1,0:T(8,128)(2,1)S(1)}, bf16[32,256]{1,0:T(8,128)(2,1)S(1)}, u32[]{:S(2)}, u32[]{:S(2)}) collective-permute-start(bf16[32,256]{1,0:T(8,128)(2,1)S(1)} %get-tuple-element.17), channel_id=1, source_target_pairs={{0,3},{1,0},{2,1},{3,2},{4,7},{5,4},{6,5},{7,6},{8,11},{9,8},{10,9... | collective-permute-start | bytes 49160 | tf_op jit(solution)/shard_map/ppermute | solution.py:314
  38.3 0.0 collective-permute-done.1.rest_1_
  38.3 0.0 collective-permute-done.2.rest_2_
  38.4 1.8 %collective-permute-done.3.rest_3_ = bf16[32,256]{1,0:T(8,128)(2,1)S(1)} collective-permute-done((bf16[32,256]{1,0:T(8,128)(2,1)S(1)}, bf16[32,256]{1,0:T(8,128)(2,1)S(1)}, u32[]{:S(2)}, u32[]{:S(2)}) %collective-permute-start.3) | collective-permute-done | bytes 16416 | tf_op jit(solution)/shard_map/ppermute | solution.py:314
  40.1 7.3 %all-to-all-done = bf16[64,8,256]{2,1,0:T(8,128)(2,1)S(1)} async-done(((bf16[64,8,256]{2,1,0:T(8,128)(2,1)}), bf16[64,8,256]{2,1,0:T(8,128)(2,1)S(1)}, u32[]{:S(2)}, u32[]{:S(2)}) %all-to-all-start) | async-done | bytes 262176 | tf_op jit(solution)/shard_map/all_to_all | solution.py:312
  47.4 0.0 copy-done.1
  47.4 0.0 copy-done.2
  47.4 0.0 copy-done.3
  47.4 0.0 copy-done.8
  47.4 0.6 copy-done.5
  48.1 0.0 copy-done.6
  48.1 0.0 copy-done.7
  48.1 3.7 %shard_map.105 = (bf16[1024,256]{1,0:T(8,128)(2,1)S(1)}, f32[544,128]{1,0:T(8,128)S(1)}) custom-call(s32[2]{0:T(128)S(1)} %pad_add_fusion.place_ref, s32[16]{0:T(128)S(1)} %copy-done.5, s32[8]{0:T(128)S(1)} %copy-done.6, s32[8]{0:T(128)S(1)} %copy-done.7, s32[1,2]{1,0:T(1,128)S(1)} %copy-done.8, bf16[1024,256]{1,0:T(8,128)(2,1)S(1)} %copy-done.1, ...), custom_call_target="tpu_custom_call" | custom-call | tf_op jit(solution)/shard_map/pallas_call | solution.py:278
  51.7 17.9 %all_to_all.20 = f32[32,1,2176]{2,1,0:T(1,128)S(1)} all-to-all(f32[32,1,2176]{2,1,0:T(1,128)S(1)} %bitcast.14), channel_id=1, replica_groups=mesh['x'=4,'z'=16,'c'=2,'y'=4] {'x','c','y'}, dimensions={0} | all-to-all | bytes 557056 | tf_op jit(solution)/shard_map/all_to_all | solution.py:294
  69.7 0.2 reduce_sum.18
  69.9 0.1 broadcast_in_dim.13
  69.9 15.2 %all_to_all.21 = f32[16,1,2176]{2,1,0:T(1,128)S(1)} all-to-all(f32[16,1,2176]{2,1,0:T(1,128)S(1)} %broadcast_in_dim.13), channel_id=1, replica_groups=mesh['x'=4,'z'=16,'c'=2,'y'=4] {'z'}, dimensions={0} | all-to-all | bytes 278528 | tf_op jit(solution)/shard_map/all_to_all | solution.py:296
  85.2 0.1 reduce_sum.19
  85.3 0.1 broadcast_in_dim.22
  85.4 15.8 %all_to_all.22 = f32[32,1,2176]{2,1,0:T(1,128)S(1)} all-to-all(f32[32,1,2176]{2,1,0:T(1,128)S(1)} %broadcast_in_dim.22), channel_id=1, replica_groups=mesh['x'=4,'z'=16,'c'=2,'y'=4] {'x','c','y'}, dimensions={0} | all-to-all | bytes 557056 | tf_op jit(solution)/shard_map/all_to_all | solution.py:298
  101.2 8.3 %shard_map.106 = (bf16[1024,256]{1,0:T(8,128)(2,1)}, f32[1,1]{1,0:T(1,128)}) custom-call(f32[544,128]{1,0:T(8,128)S(1)} %bitcast.12, bf16[1024,256]{1,0:T(8,128)(2,1)S(1)} %get-tuple-element.19.hidden_ref), custom_call_target="tpu_custom_call" | custom-call | tf_op jit(solution)/shard_map/pallas_call | solution.py:161
  (11 shorter events, 0.0 us)
Async XLA Ops:
  0.7 0.7 copy-start.4
  0.7 0.7 copy-start.9
  1.4 1.0 copy-start
  3.8 9.9 %collective-permute-start = (bf16[512,256]{1,0:T(8,128)(2,1)S(1)}, bf16[512,256]{1,0:T(8,128)(2,1)S(1)}, u32[]{:S(2)}, u32[]{:S(2)}) collective-permute-start(bf16[512,256]{1,0:T(8,128)(2,1)S(1)} %get-tuple-element.13), channel_id=1, source_target_pairs={{0,4},{4,0},{1,5},{5,1},{2,6},{6,2},{3,7},{7,3},{8,12},{12,8},{9,1... | collective-permute-start | bytes 786440 | tf_op jit(solution)/shard_map/ppermute | solution.py:309
  13.8 33.7 %copy-start.1 = (bf16[1024,256]{1,0:T(8,128)(2,1)S(1)}, bf16[1024,256]{1,0:T(8,128)(2,1)}, u32[]{:S(2)}) copy-start(bf16[1024,256]{1,0:T(8,128)(2,1)} %features_ref.3) | copy-start | bytes 1572868
  13.8 33.7 %copy-start.2 = (bf16[16,128,128]{2,1,0:T(8,128)(2,1)S(1)}, bf16[16,128,128]{2,1,0:T(8,128)(2,1)}, u32[]{:S(2)}) copy-start(bf16[16,128,128]{2,1,0:T(8,128)(2,1)} %tile_ref.1) | copy-start | bytes 1572868
  14.6 32.9 %copy-start.3 = (bf16[256,256]{1,0:T(8,128)(2,1)S(1)}, bf16[256,256]{1,0:T(8,128)(2,1)}, u32[]{:S(2)}) copy-start(bf16[256,256]{1,0:T(8,128)(2,1)} %weight_ref.1) | copy-start | bytes 393220
  14.6 32.9 %copy-start.8 = (s32[1,2]{1,0:T(1,128)S(1)}, s32[1,2]{1,0:T(1,128)}, u32[]{:S(2)}) copy-start(s32[1,2]{1,0:T(1,128)} %live_ref.1) | copy-start | bytes 28
  14.6 32.8 %all-to-all-start = ((bf16[64,8,256]{2,1,0:T(8,128)(2,1)}), bf16[64,8,256]{2,1,0:T(8,128)(2,1)S(1)}, u32[]{:S(2)}, u32[]{:S(2)}) async-start(bf16[64,8,256]{2,1,0:T(8,128)(2,1)} %bitcast_select_fusion), calls=%async_computation | async-start | bytes 524288 | tf_op jit(solution)/shard_map/all_to_all | solution.py:312
  27.6 10.7 %collective-permute-start.1 = (bf16[32,256]{1,0:T(8,128)(2,1)S(1)}, bf16[32,256]{1,0:T(8,128)(2,1)S(1)}, u32[]{:S(2)}, u32[]{:S(2)}) collective-permute-start(bf16[32,256]{1,0:T(8,128)(2,1)S(1)} %get-tuple-element.15), channel_id=1, source_target_pairs={{0,1},{1,2},{2,3},{3,0},{4,5},{5,6},{6,7},{7,4},{8,9},{9,10},{10,1... | collective-permute-start | bytes 49160 | tf_op jit(solution)/shard_map/ppermute | solution.py:314
  30.8 7.5 %collective-permute-start.2 = (bf16[32,256]{1,0:T(8,128)(2,1)S(1)}, bf16[32,256]{1,0:T(8,128)(2,1)S(1)}, u32[]{:S(2)}, u32[]{:S(2)}) collective-permute-start(bf16[32,256]{1,0:T(8,128)(2,1)S(1)} %get-tuple-element.16), channel_id=1, source_target_pairs={{0,2},{1,3},{2,0},{3,1},{4,6},{5,7},{6,4},{7,5},{8,10},{9,11},{10,... | collective-permute-start | bytes 49160 | tf_op jit(solution)/shard_map/ppermute | solution.py:314
  35.4 4.8 %collective-permute-start.3 = (bf16[32,256]{1,0:T(8,128)(2,1)S(1)}, bf16[32,256]{1,0:T(8,128)(2,1)S(1)}, u32[]{:S(2)}, u32[]{:S(2)}) collective-permute-start(bf16[32,256]{1,0:T(8,128)(2,1)S(1)} %get-tuple-element.17), channel_id=1, source_target_pairs={{0,3},{1,0},{2,1},{3,2},{4,7},{5,4},{6,5},{7,6},{8,11},{9,8},{10,9... | collective-permute-start | bytes 49160 | tf_op jit(solution)/shard_map/ppermute | solution.py:314
  47.4 0.7 copy-start.5
  47.4 0.7 copy-start.6
  47.4 0.7 copy-start.7

commit v4 on v3

--- a/solution.py
+++ b/solution.py
@@ -18,6 +18,7 @@
 
 VMEM = pl.BlockSpec(memory_space=pltpu.VMEM)
 SMEM = pl.BlockSpec(memory_space=pltpu.SMEM)
+HBM = pl.BlockSpec(memory_space=pltpu.HBM)
 
 
 def iota(shape, dim):
@@ -185,79 +186,136 @@
     return [both[:, :LANES], both[:, LANES:], jnp.where(corner, square_sum, spare)]
 
 
-def gather_kernel(place_ref, features_ref, far_index_ref, near_index_ref, far_ref, turned_ref, near_own_ref, *near_refs):
-    source, width = features_ref.shape
+def gather_kernel(features_hbm, far_hbm, near_hbm, *rest):
+    *outs, features_ref, far_index_ref, near_index_ref, far_ref, near_ref, in_sems, far_sems, near_sems = rest
+    far_out, *near_outs = outs
+    arrivals = [
+        pltpu.make_async_copy(source, target, in_sems.at[i])
+        for i, (source, target) in enumerate(
+            ((far_hbm, far_index_ref), (near_hbm, near_index_ref), (features_hbm, features_ref))
+        )
+    ]
+    for copy in arrivals:
+        copy.start()
+    source = features_ref.shape[0]
     lane = iota((LANES, LANES), 1)
-    features = features_ref[...]
-
-    def rows_at(index):
+
+    def picks_of(index):
         wanted = jnp.broadcast_to(index.astype(jnp.float32), (LANES, LANES)).T.astype(jnp.int32)
         picks = [
             jnp.where(wanted == lane + LANES * s, 1.0, 0.0).astype(jnp.bfloat16) for s in range(source // LANES)
         ]
-        return contract(jnp.concatenate(picks, 1), features, ((1,), (0,)))
-
-    for r in range(far_index_ref.shape[0]):
-        picked = rows_at(far_index_ref[r : r + 1, :])
-        here = slice(LANES * r, LANES * r + LANES)
-        far_ref[here, :] = picked.astype(far_ref.dtype)
-        turned = pltpu.roll(picked.reshape(LANES // SUB, SUB, width), SUB // 2, 1)
-        turned_ref[here, :] = turned.reshape(LANES, width).astype(turned_ref.dtype)
-    picked = rows_at(near_index_ref[...]).astype(near_own_ref.dtype)
-    peers = 1 + len(near_refs)
+        return jnp.concatenate(picks, 1)
+
+    arrivals[0].wait()
+    arrivals[1].wait()
+    far_picks = [picks_of(far_index_ref[r : r + 1, :]) for r in range(far_index_ref.shape[0])]
+    near_picks = picks_of(near_index_ref[...])
+    arrivals[2].wait()
+    features = features_ref[...]
+    leaving = []
+    for r, picks in enumerate(far_picks):
+        here = pl.ds(LANES * r, LANES)
+        far_ref[here, :] = contract(picks, features, ((1,), (0,))).astype(far_ref.dtype)
+        leaving.append(pltpu.make_async_copy(far_ref.at[here], far_out.at[here], far_sems.at[r]))
+        leaving[-1].start()
+    near_ref[...] = contract(near_picks, features, ((1,), (0,))).astype(near_ref.dtype)
+    peers = len(near_outs)
     block = LANES // peers
-    for k, ref in enumerate((near_own_ref, *near_refs)):
-        for q in range(peers):
-            @pl.when(lax.rem(place_ref[1] + k, peers) == q)
-            def _(ref=ref, q=q):
-                ref[...] = picked[block * q : block * q + block]
-
-
-def gather(place, features, far_index, near_index, peers):
+    y = lax.axis_index("y")
+    for k, out in enumerate(near_outs):
+        first = pl.multiple_of(lax.rem(y + k, peers) * block, block)
+        leaving.append(pltpu.make_async_copy(near_ref.at[pl.ds(first, block)], out, near_sems.at[k]))
+        leaving[-1].start()
+    for copy in leaving:
+        copy.wait()
+
+
+def gather(features, far_index, near_index, peers):
     width, dtype = features.shape[1], features.dtype
     far = jax.ShapeDtypeStruct((far_index.size, width), dtype)
     near = jax.ShapeDtypeStruct((near_index.size // peers, width), dtype)
+    far_index, near_index = far_index.reshape(-1, LANES), near_index.reshape(-1, LANES)
     return pl.pallas_call(
         gather_kernel,
-        out_shape=(far, far) + (near,) * peers,
-        in_specs=[SMEM, VMEM, VMEM, VMEM],
-        out_specs=(VMEM,) * (2 + peers),
-        compiler_params=pltpu.CompilerParams(vmem_limit_bytes=24 * 2**20),
-    )(place, features, far_index.reshape(-1, LANES), near_index.reshape(-1, LANES))
+        out_shape=(far,) + (near,) * peers,
+        in_specs=[HBM] * 3,
+        out_specs=(HBM,) * (1 + peers),
+        scratch_shapes=[
+            pltpu.VMEM(features.shape, dtype),
+            pltpu.VMEM(far_index.shape, jnp.int32),
+            pltpu.VMEM(near_index.shape, jnp.int32),
+            pltpu.VMEM(far.shape, dtype),
+            pltpu.VMEM((near_index.size, width), dtype),
+            pltpu.SemaphoreType.DMA((3,)),
+            pltpu.SemaphoreType.DMA((far_index.shape[0],)),
+            pltpu.SemaphoreType.DMA((peers,)),
+        ],
+        compiler_params=pltpu.CompilerParams(vmem_limit_bytes=62 * 2**20),
+    )(features, far_index, near_index)
+
+
+def add_tile(sum_ref, dst_ref, slot, weights, source_ref, index):
+    tile = weights.shape[0]
+    to = pl.ds(pl.multiple_of(dst_ref[slot] * tile, tile), tile)
+    source = source_ref[pl.ds(pl.multiple_of(index * tile, tile), tile), :]
+    sum_ref[to, :] += contract(weights, source, ((1,), (0,)))
+
+
+def inner_kernel(dst_ref, inner_ref, outer_ref, live_ref, features_ref, tile_ref, sum_ref, square_ref):
+    sum_ref[...] = jnp.zeros_like(sum_ref)
+    for k in range(inner_ref.shape[0]):
+        @pl.when(k < live_ref[0, 0])
+        def _(k=k):
+            add_tile(sum_ref, dst_ref, k, tile_ref[k], features_ref, inner_ref[k])
+
+    wide = features_ref[...].astype(jnp.float32)
+    square = jnp.sum((wide * wide).reshape(-1, SUB, wide.shape[1]), 0)
+    square_ref[...] = sum(square[:, i : i + LANES] for i in range(0, wide.shape[1], LANES))
+
+
+def inner_sums(dst, inner, outer, live, features, tiles):
+    rows, width = features.shape
+    return pl.pallas_call(
+        inner_kernel,
+        out_shape=(
+            jax.ShapeDtypeStruct((rows, width), jnp.float32),
+            jax.ShapeDtypeStruct((SUB, LANES), jnp.float32),
+        ),
+        in_specs=[SMEM] * 4 + [VMEM] * 2,
+        out_specs=(VMEM, VMEM),
+        compiler_params=pltpu.CompilerParams(vmem_limit_bytes=16 * 2**20),
+        cost_estimate=pl.CostEstimate(flops=10**8, bytes_accessed=2 * 10**6, transcendentals=0),
+    )(dst, inner, outer, live, features, tiles)
 
 
 def layer_kernel(
-    place_ref, dst_ref, inner_ref, outer_ref, live_ref, features_ref, far_ref, tile_ref, weight_ref, *rest
+    dst_ref, outer_ref, live_ref, features_ref, own_ref, crossed_ref, tile_ref, weight_ref, inner_sum_ref,
+    square_ref, *rest,
 ):
-    *near_refs, hidden_ref, parts_ref, sum_ref, near_ref = rest
+    *near_refs, hidden_ref, parts_ref, sum_ref, near_ref, far_ref = rest
+    own, crossed = (
+        ref[...].astype(jnp.float32).reshape(-1, SUB, ref.shape[1]) for ref in (own_ref, crossed_ref)
+    )
+    core = jnp.where(iota(own.shape, 1) >= SUB // 2, 1, 0)
+    far = jnp.where(core == lax.axis_index("c"), own, pltpu.roll(crossed, SUB // 2, 1))
+    far_ref[...] = far.reshape(far_ref.shape).astype(far_ref.dtype)
     peers = len(near_refs)
     block = near_ref.shape[0] // peers
     for k, ref in enumerate(near_refs):
-        at = lax.rem(place_ref[1] + peers - k, peers)
+        at = lax.rem(lax.axis_index("y") + peers - k, peers)
         near_ref[pl.ds(pl.multiple_of(at * block, block), block), :] = ref[...]
-    slots, tile = inner_ref.shape[0], tile_ref.shape[1]
+    slots, tile = outer_ref.shape[0], tile_ref.shape[1]
     far_tiles = far_ref.shape[0] // tile
-    sum_ref[...] = jnp.zeros_like(sum_ref)
-
-    def add(c, source):
-        to = pl.ds(pl.multiple_of(dst_ref[c] * tile, tile), tile)
-        sum_ref[to, :] += contract(tile_ref[c], source, ((1,), (0,)))
-
-    def rows_of(ref, index):
-        return ref[pl.ds(pl.multiple_of(index * tile, tile), tile), :]
-
+    sum_ref[...] = inner_sum_ref[...]
     for k in range(slots):
-        @pl.when(k < live_ref[0, 0])
-        def _(k=k):
-            add(k, rows_of(features_ref, inner_ref[k]))
-
         @pl.when((k < live_ref[0, 1]) & (outer_ref[k] < far_tiles))
         def _(k=k):
-            add(slots + k, rows_of(far_ref, outer_ref[k]))
+            add_tile(sum_ref, dst_ref, slots + k, tile_ref[slots + k], far_ref, outer_ref[k])
 
         @pl.when((k < live_ref[0, 1]) & (outer_ref[k] >= far_tiles))
         def _(k=k):
-            add(slots + k, rows_of(near_ref, outer_ref[k] - far_tiles))
+            add_tile(sum_ref, dst_ref, slots + k, tile_ref[slots + k], near_ref, outer_ref[k] - far_tiles)
 
     projected = contract(sum_ref[...].astype(jnp.bfloat16), weight_ref[...], ((1,), (0,)))
     features = features_ref[...]
@@ -267,12 +325,12 @@
     gram = contract(hidden, hidden, ((0,), (0,)))
     cross = contract(hidden, features, ((0,), (0,)))
     first = 0
-    for part in pack(gram, cross, jnp.sum(wide * wide)):
+    for part in pack(gram, cross, jnp.sum(square_ref[...])):
         parts_ref[first : first + part.shape[0], :] = part
         first += part.shape[0]
 
 
-def layer(place, dst, inner, outer, live, features, far, tiles, weight, near):
+def layer(dst, outer, live, features, far, crossed, tiles, weight, inner, near):
     rows, width = features.shape
     near_rows = sum(n.shape[0] for n in near)
     return pl.pallas_call(
@@ -281,11 +339,15 @@
             jax.ShapeDtypeStruct((rows, width), jnp.bfloat16),
             jax.ShapeDtypeStruct((2 * width + width // SUB, LANES), jnp.float32),
         ),
-        in_specs=[SMEM] * 5 + [VMEM] * (4 + len(near)),
+        in_specs=[SMEM] * 3 + [VMEM] * (7 + len(near)),
         out_specs=(VMEM, VMEM),
-        scratch_shapes=[pltpu.VMEM((rows, width), jnp.float32), pltpu.VMEM((near_rows, width), features.dtype)],
-        compiler_params=pltpu.CompilerParams(vmem_limit_bytes=32 * 2**20),
-    )(place, dst, inner, outer, live, features, far, tiles, weight, *near)
+        scratch_shapes=[
+            pltpu.VMEM((rows, width), jnp.float32),
+            pltpu.VMEM((near_rows, width), features.dtype),
+            pltpu.VMEM(far.shape, features.dtype),
+        ],
+        compiler_params=pltpu.CompilerParams(vmem_limit_bytes=24 * 2**20),
+    )(dst, outer, live, features, far, crossed, tiles, weight, *inner, *near)
 
 
 def sum_over_all(parts):
@@ -302,19 +364,17 @@
     features, weight, send_far, send_near, tile_dst, inner_src, outer_src, tile_live, tile_weight
 ):
     rows, width = features.shape
-    core, y = lax.axis_index("c"), lax.axis_index("y")
     peers = lax.axis_size("y")
-    place = jnp.stack([core, y]).astype(jnp.int32)
-    far, turned, *near = gather(place, features, send_far, send_near, peers)
-    crossed = lax.ppermute(turned, "c", [(0, 1), (1, 0)])
-    upper = iota((1, SUB, 1), 1) >= SUB // 2
-    mixed = jnp.where(upper == (core == 1), far.reshape(-1, SUB, width), crossed.reshape(-1, SUB, width))
-    far = lax.all_to_all(mixed, ("x", "z"), 0, 0, tiled=True).reshape(-1, width)
+    far, *near = gather(features, send_far, send_near, peers)
+    far = lax.all_to_all(far.reshape(-1, SUB, width), ("x", "z"), 0, 0, tiled=True).reshape(-1, width)
     near = near[:1] + [
         lax.ppermute(near[k], "y", [(i, (i + k) % peers) for i in range(peers)]) for k in range(1, peers)
     ]
+    inner = inner_sums(tile_dst, inner_src, outer_src, tile_live, features, tile_weight)
+    far, near, inner = lax.optimization_barrier((far, near, inner))
+    crossed = lax.ppermute(far, "c", [(0, 1), (1, 0)])
     hidden, parts = layer(
-        place, tile_dst, inner_src, outer_src, tile_live, features, far, tile_weight, weight, near
+        tile_dst, outer_src, tile_live, features, far, crossed, tile_weight, weight, inner, near
     )
     parts = sum_over_all(parts)
     vertex_count = rows * lax.axis_size(DOM) * lax.axis_size("y")

time: 110 us -> 107 us (0.973)
  waiting for transfers between devices: 10.2 us -> 7.33 us
  starting transfers between devices: 32.5 us -> 34.9 us
  local copies, waits for them, and re-layouts: 2.61 us -> 0.26 us
  Pallas kernels: 13.3 us -> 14.9 us
    all_to_all x1, starting transfers between devices: 13 us -> 19.1 us  [body(): lax.all_to_all(far.reshape(-1, SUB, width), ('x', 'z'), 0, 0, tiled=True)]
    ppermute x1, starting transfers between devices: 8.78 us -> 4.78 us  [body(): crossed = lax.ppermute(far, 'c', [(0, 1), (1, 0)])]
    pallas_call x1 -> x2, Pallas kernels: 1.38 us -> 4.12 us  [the longest x1 2.41 us: gather(): pl.pallas_call(gather_kernel, out_shape=(far,) + (near,) * peers, in_spec...]
    unnamed x20 -> x16, local copies, waits for them, and re-layouts: 2.39 us -> 0.04 us
    all_to_all x1, blocking collectives: 17.9 us -> 16.3 us  [sum_over_all(): own = jnp.sum(lax.all_to_all(pieces, near, 0, 0, tiled=True), 0)]
    ppermute x3, waiting for transfers between devices: 1.78 us -> 0.2 us  [body(): lax.ppermute(near[k], 'y', [(i, (i + k) % peers) for i in range(peers)])]
    all_to_all x1, waiting for transfers between devices: 7.27 us -> 5.99 us  [body(): lax.all_to_all(far.reshape(-1, SUB, width), ('x', 'z'), 0, 0, tiled=True)]
    pallas_call x1, Pallas kernels: 3.65 us -> 2.45 us  [layer(): pl.pallas_call(layer_kernel, out_shape=(jax.ShapeDtypeStruct((rows, width...]
  transfers between devices with their start and end apart: 5 -> 5, of which waited for: 3 -> 3; matrix products, arithmetic and copies ran while one was open for 0% -> 0% of each run, Pallas kernels for 0% -> 2%
where the time goes in v4:
time: 107 us
  blocking collectives  48.4 us (45%)
  starting transfers between devices  34.9 us (33%)
  Pallas kernels  14.9 us (14%)
  waiting for transfers between devices  7.33 us (7%)
    all_to_all x1, starting transfers between devices, body(): lax.all_to_all(far.reshape(-1, SUB, width), ('x', 'z'), 0, 0, tiled=True)  19.1 us
    all_to_all x1, blocking collectives, sum_over_all(): own = jnp.sum(lax.all_to_all(pieces, near, 0, 0, tiled=True), 0)  16.3 us
    all_to_all x1, blocking collectives, sum_over_all(): own = jnp.sum(lax.all_to_all(own, far, 0, 0, tiled=True), 0)  16.2 us
    all_to_all x1, blocking collectives, sum_over_all(): return lax.all_to_all(own, near, 0, 0, tiled=True).reshape(parts.shape)  15.8 us
    ppermute x3, starting transfers between devices, body(): lax.ppermute(near[k], 'y', [(i, (i + k) % peers) for i in range(peers)])  11 us
    pallas_call x1, Pallas kernels, whiten(): pl.pallas_call(functools.partial(whiten_kernel, vertex_count), out_shape=...  8.29 us
    all_to_all x1, waiting for transfers between devices, body(): lax.all_to_all(far.reshape(-1, SUB, width), ('x', 'z'), 0, 0, tiled=True)  5.99 us
    ppermute x1, starting transfers between devices, body(): crossed = lax.ppermute(far, 'c', [(0, 1), (1, 0)])  4.78 us
  transfers between devices with their start and end apart: 5, of which 3 were waited for; matrix products, arithmetic and copies ran while one was open for 0% of the time, Pallas kernels for 2%

profile of v4, /device:TPU:1, one launch (start us, length us, event | category | flops | bytes accessed | tf_op | source)
XLA Modules:
  0.0 106.8 jit_solution(1005478976169734461)
XLA Ops:
  0.6 0.0 copy-start
  0.6 0.0 copy-start.1
  0.7 2.4 %shard_map.104 = (bf16[512,256]{1,0:T(8,128)(2,1)}, bf16[32,256]{1,0:T(8,128)(2,1)}, bf16[32,256]{1,0:T(8,128)(2,1)}, bf16[32,256]{1,0:T(8,128)(2,1)}, bf16[32,256]{1,0:T(8,128)(2,1)}) custom-call(bf16[1024,256]{1,0:T(8,128)(2,1)} %features_ref.3, s32[4,128]{1,0:T(4,128)} %bitcast.12, s32[1,128]{1,0:T(1,128)} %bitcast.13), custom_call_target="tpu_custom_call" | custom-call | tf_op jit(solution)/shard_map/pallas_call | solution.py:239
  3.1 19.1 %all-to-all-start = ((bf16[64,8,256]{2,1,0:T(8,128)(2,1)}), bf16[64,8,256]{2,1,0:T(8,128)(2,1)S(1)}, u32[]{:S(2)}, u32[]{:S(2)}) async-start(bf16[64,8,256]{2,1,0:T(8,128)(2,1)} %bitcast.11), calls=%async_computation | async-start | bytes 524288 | tf_op jit(solution)/shard_map/all_to_all | solution.py:369
  22.2 3.2 %collective-permute-start = (bf16[32,256]{1,0:T(8,128)(2,1)}, bf16[32,256]{1,0:T(8,128)(2,1)S(1)}, u32[]{:S(2)}, u32[]{:S(2)}) collective-permute-start(bf16[32,256]{1,0:T(8,128)(2,1)} %get-tuple-element.22), channel_id=1, source_target_pairs={{0,1},{1,2},{2,3},{3,0},{4,5},{5,6},{6,7},{7,4},{8,9},{9,10},{10,1... | collective-permute-start | bytes 49160 | tf_op jit(solution)/shard_map/ppermute | solution.py:371
  25.4 0.0 copy-start.7
  25.4 0.0 copy-start.4
  25.4 0.0 copy-start.5
  25.4 0.0 copy-start.6
  25.5 4.7 %collective-permute-start.1 = (bf16[32,256]{1,0:T(8,128)(2,1)}, bf16[32,256]{1,0:T(8,128)(2,1)S(1)}, u32[]{:S(2)}, u32[]{:S(2)}) collective-permute-start(bf16[32,256]{1,0:T(8,128)(2,1)} %get-tuple-element.23), channel_id=1, source_target_pairs={{0,2},{1,3},{2,0},{3,1},{4,6},{5,7},{6,4},{7,5},{8,10},{9,11},{10,... | collective-permute-start | bytes 49160 | tf_op jit(solution)/shard_map/ppermute | solution.py:371
  30.1 0.0 copy-start.2
  30.1 3.1 %collective-permute-start.2 = (bf16[32,256]{1,0:T(8,128)(2,1)}, bf16[32,256]{1,0:T(8,128)(2,1)S(1)}, u32[]{:S(2)}, u32[]{:S(2)}) collective-permute-start(bf16[32,256]{1,0:T(8,128)(2,1)} %get-tuple-element.24), channel_id=1, source_target_pairs={{0,3},{1,0},{2,1},{3,2},{4,7},{5,4},{6,5},{7,6},{8,11},{9,8},{10,9... | collective-permute-start | bytes 49160 | tf_op jit(solution)/shard_map/ppermute | solution.py:371
  33.2 0.0 copy-done
  33.3 0.0 copy-done.1
  33.3 0.0 copy-done.7
  33.3 1.7 %shard_map.105 = (f32[1024,256]{1,0:T(8,128)S(1)}, f32[8,128]{1,0:T(8,128)S(1)}) custom-call(s32[16]{0:T(128)S(1)} %copy-done.4, s32[8]{0:T(128)S(1)} %copy-done.7, s32[8]{0:T(128)S(1)} %copy-done.5, s32[1,2]{1,0:T(1,128)S(1)} %copy-done.6, bf16[1024,256]{1,0:T(8,128)(2,1)S(1)} %copy-done, bf16[16,128,128]{2,1,0:T(8,128)(2,1)S(1)} %copy-done.1), custom_call_target="tpu_custom_call" | custom-call | flops 100000000 | bytes 2000000 | tf_op jit(solution)/shard_map/pallas_call | solution.py:279
  35.0 0.0 collective-permute-done.rest_1_
  35.0 0.0 collective-permute-done.1.rest_2_
  35.1 0.2 collective-permute-done.2.rest_3_
  35.3 6.0 %all-to-all-done = bf16[64,8,256]{2,1,0:T(8,128)(2,1)S(1)} async-done(((bf16[64,8,256]{2,1,0:T(8,128)(2,1)}), bf16[64,8,256]{2,1,0:T(8,128)(2,1)S(1)}, u32[]{:S(2)}, u32[]{:S(2)}) %all-to-all-start) | async-done | bytes 262176 | tf_op jit(solution)/shard_map/all_to_all | solution.py:369
  41.2 4.8 %collective-permute-start.3 = (bf16[512,256]{1,0:T(8,128)(2,1)S(1)}, bf16[512,256]{1,0:T(8,128)(2,1)S(1)}, u32[]{:S(2)}, u32[]{:S(2)}) collective-permute-start(bf16[512,256]{1,0:T(8,128)(2,1)S(1)} %bitcast.8), channel_id=1, source_target_pairs={{0,4},{4,0},{1,5},{5,1},{2,6},{6,2},{3,7},{7,3},{8,12},{12,8},{9,1... | collective-permute-start | bytes 786440 | tf_op jit(solution)/shard_map/ppermute | solution.py:375
  46.0 1.1 %collective-permute-done.3.crossed_ref = bf16[512,256]{1,0:T(8,128)(2,1)S(1)} collective-permute-done((bf16[512,256]{1,0:T(8,128)(2,1)S(1)}, bf16[512,256]{1,0:T(8,128)(2,1)S(1)}, u32[]{:S(2)}, u32[]{:S(2)}) %collective-permute-start.3) | collective-permute-done | bytes 262176 | tf_op jit(solution)/shard_map/ppermute | solution.py:375
  47.2 0.0 copy-done.3
  47.2 2.5 %shard_map.106 = (bf16[1024,256]{1,0:T(8,128)(2,1)S(1)}, f32[544,128]{1,0:T(8,128)S(1)}) custom-call(s32[16]{0:T(128)S(1)} %copy-done.4, s32[8]{0:T(128)S(1)} %copy-done.5, s32[1,2]{1,0:T(1,128)S(1)} %copy-done.6, bf16[1024,256]{1,0:T(8,128)(2,1)S(1)} %copy-done, bf16[512,256]{1,0:T(8,128)(2,1)S(1)} %bitcast.9, ...), custom_call_target="tpu_custom_call" | custom-call | tf_op jit(solution)/shard_map/pallas_call | solution.py:336
  49.6 16.3 %all_to_all.20 = f32[32,1,2176]{2,1,0:T(1,128)S(1)} all-to-all(f32[32,1,2176]{2,1,0:T(1,128)S(1)} %bitcast.10), channel_id=1, replica_groups=mesh['x'=4,'z'=16,'c'=2,'y'=4] {'x','c','y'}, dimensions={0} | all-to-all | bytes 557056 | tf_op jit(solution)/shard_map/all_to_all | solution.py:356
  65.9 0.2 reduce_sum.18
  66.1 0.1 broadcast_in_dim.4
  66.2 16.2 %all_to_all.21 = f32[16,1,2176]{2,1,0:T(1,128)S(1)} all-to-all(f32[16,1,2176]{2,1,0:T(1,128)S(1)} %broadcast_in_dim.4), channel_id=1, replica_groups=mesh['x'=4,'z'=16,'c'=2,'y'=4] {'z'}, dimensions={0} | all-to-all | bytes 278528 | tf_op jit(solution)/shard_map/all_to_all | solution.py:358
  82.4 0.1 reduce_sum.19
  82.5 0.1 broadcast_in_dim.5
  82.7 15.8 %all_to_all.22 = f32[32,1,2176]{2,1,0:T(1,128)S(1)} all-to-all(f32[32,1,2176]{2,1,0:T(1,128)S(1)} %broadcast_in_dim.5), channel_id=1, replica_groups=mesh['x'=4,'z'=16,'c'=2,'y'=4] {'x','c','y'}, dimensions={0} | all-to-all | bytes 557056 | tf_op jit(solution)/shard_map/all_to_all | solution.py:360
  98.5 8.3 %shard_map.107 = (bf16[1024,256]{1,0:T(8,128)(2,1)}, f32[1,1]{1,0:T(1,128)}) custom-call(f32[544,128]{1,0:T(8,128)S(1)} %bitcast.7, bf16[1024,256]{1,0:T(8,128)(2,1)S(1)} %get-tuple-element.35.hidden_ref), custom_call_target="tpu_custom_call" | custom-call | tf_op jit(solution)/shard_map/pallas_call | solution.py:162
  (5 shorter events, 0.0 us)
Async XLA Ops:
  0.6 32.6 %copy-start = (bf16[1024,256]{1,0:T(8,128)(2,1)S(1)}, bf16[1024,256]{1,0:T(8,128)(2,1)}, u32[]{:S(2)}) copy-start(bf16[1024,256]{1,0:T(8,128)(2,1)} %features_ref.3) | copy-start | bytes 1572868
  0.6 32.6 %copy-start.1 = (bf16[16,128,128]{2,1,0:T(8,128)(2,1)S(1)}, bf16[16,128,128]{2,1,0:T(8,128)(2,1)}, u32[]{:S(2)}) copy-start(bf16[16,128,128]{2,1,0:T(8,128)(2,1)} %tile_ref.3) | copy-start | bytes 1572868
  3.1 38.2 %all-to-all-start = ((bf16[64,8,256]{2,1,0:T(8,128)(2,1)}), bf16[64,8,256]{2,1,0:T(8,128)(2,1)S(1)}, u32[]{:S(2)}, u32[]{:S(2)}) async-start(bf16[64,8,256]{2,1,0:T(8,128)(2,1)} %bitcast.11), calls=%async_computation | async-start | bytes 524288 | tf_op jit(solution)/shard_map/all_to_all | solution.py:369
  22.2 12.8 %collective-permute-start = (bf16[32,256]{1,0:T(8,128)(2,1)}, bf16[32,256]{1,0:T(8,128)(2,1)S(1)}, u32[]{:S(2)}, u32[]{:S(2)}) collective-permute-start(bf16[32,256]{1,0:T(8,128)(2,1)} %get-tuple-element.22), channel_id=1, source_target_pairs={{0,1},{1,2},{2,3},{3,0},{4,5},{5,6},{6,7},{7,4},{8,9},{9,10},{10,1... | collective-permute-start | bytes 49160 | tf_op jit(solution)/shard_map/ppermute | solution.py:371
  25.4 7.9 %copy-start.7 = (s32[8]{0:T(128)S(1)}, s32[8]{0:T(128)}, u32[]{:S(2)}) copy-start(s32[8]{0:T(128)} %inner_ref.1) | copy-start | bytes 100
  25.4 7.9 %copy-start.4 = (s32[16]{0:T(128)S(1)}, s32[16]{0:T(128)}, u32[]{:S(2)}) copy-start(s32[16]{0:T(128)} %dst_ref.3) | copy-start | bytes 196
  25.4 7.9 %copy-start.5 = (s32[8]{0:T(128)S(1)}, s32[8]{0:T(128)}, u32[]{:S(2)}) copy-start(s32[8]{0:T(128)} %outer_ref.3) | copy-start | bytes 100
  25.4 7.9 %copy-start.6 = (s32[1,2]{1,0:T(1,128)S(1)}, s32[1,2]{1,0:T(1,128)}, u32[]{:S(2)}) copy-start(s32[1,2]{1,0:T(1,128)} %live_ref.3) | copy-start | bytes 28
  25.5 9.6 %collective-permute-start.1 = (bf16[32,256]{1,0:T(8,128)(2,1)}, bf16[32,256]{1,0:T(8,128)(2,1)S(1)}, u32[]{:S(2)}, u32[]{:S(2)}) collective-permute-start(bf16[32,256]{1,0:T(8,128)(2,1)} %get-tuple-element.23), channel_id=1, source_target_pairs={{0,2},{1,3},{2,0},{3,1},{4,6},{5,7},{6,4},{7,5},{8,10},{9,11},{10,... | collective-permute-start | bytes 49160 | tf_op jit(solution)/shard_map/ppermute | solution.py:371
  30.1 17.1 %copy-start.2 = (bf16[256,256]{1,0:T(8,128)(2,1)S(1)}, bf16[256,256]{1,0:T(8,128)(2,1)}, u32[]{:S(2)}) copy-start(bf16[256,256]{1,0:T(8,128)(2,1)} %weight_ref.1) | copy-start | bytes 393220
  30.1 5.1 %collective-permute-start.2 = (bf16[32,256]{1,0:T(8,128)(2,1)}, bf16[32,256]{1,0:T(8,128)(2,1)S(1)}, u32[]{:S(2)}, u32[]{:S(2)}) collective-permute-start(bf16[32,256]{1,0:T(8,128)(2,1)} %get-tuple-element.24), channel_id=1, source_target_pairs={{0,3},{1,0},{2,1},{3,2},{4,7},{5,4},{6,5},{7,6},{8,11},{9,8},{10,9... | collective-permute-start | bytes 49160 | tf_op jit(solution)/shard_map/ppermute | solution.py:371
  33.3 13.9 %copy-start.3 = (bf16[32,256]{1,0:T(8,128)(2,1)S(1)}, bf16[32,256]{1,0:T(8,128)(2,1)}, u32[]{:S(2)}) copy-start(bf16[32,256]{1,0:T(8,128)(2,1)} %get-tuple-element.30.rest_0_) | copy-start | bytes 49156
  41.2 5.9 %collective-permute-start.3 = (bf16[512,256]{1,0:T(8,128)(2,1)S(1)}, bf16[512,256]{1,0:T(8,128)(2,1)S(1)}, u32[]{:S(2)}, u32[]{:S(2)}) collective-permute-start(bf16[512,256]{1,0:T(8,128)(2,1)S(1)} %bitcast.8), channel_id=1, source_target_pairs={{0,4},{4,0},{1,5},{5,1},{2,6},{6,2},{3,7},{7,3},{8,12},{12,8},{9,1... | collective-permute-start | bytes 786440 | tf_op jit(solution)/shard_map/ppermute | solution.py:375

commit v5 on v4

--- a/solution.py
+++ b/solution.py
@@ -12,7 +12,7 @@
 DOM = ("x", "z", "c")
 
 EPSILON = 1e-05
-PANEL = 32
+PANEL = 64
 SUB = 8
 LANES = 128
 
@@ -37,28 +37,37 @@
     return high, middle, low
 
 
-def eliminate_panel(rows, near, first_lane, width):
-    groups = PANEL // SUB
-    rows, near = list(rows), list(near)
+def eliminate_panel(rows, first_lane):
+    rows = list(rows)
+    groups, width = len(rows), rows[0].shape[1]
     lane = iota((SUB, width), 1)
     sub = iota((SUB, width), 0)
     sub_lane = iota((SUB, LANES), 0)
     pivots = [None] * groups
     full = (SUB, LANES)
+
+    def widened(x):
+        return jnp.concatenate([x] * (width // LANES), 1)
+
     for b in range(groups):
         start = first_lane + SUB * b
-        in_block = (lane >= start) & (lane < start + SUB)
-        unit = jnp.where(lane - start == sub, 1.0, 0.0)
-        rows[b] = jnp.where(in_block, unit, rows[b])
-        for g in range(b + 1, groups):
-            rows[g] = jnp.where(in_block, 0.0, rows[g])
+        part = slice(start // LANES * LANES, start // LANES * LANES + LANES)
         column = [
-            {g: jnp.take_along_axis(near[g], jnp.full(full, SUB * b + k, jnp.int32), 1, mode='promise_in_bounds') for g in range(b, groups)}
+            {
+                g: jnp.take_along_axis(
+                    rows[g][:, part], jnp.full(full, start % LANES + k, jnp.int32), 1, mode="promise_in_bounds"
+                )
+                for g in range(b, groups)
+            }
             for k in range(SUB)
         ]
         entry = {
             (m, k): jnp.broadcast_to(column[k][b][m : m + 1, :], full) for k in range(SUB) for m in range(k, SUB)
         }
+        in_block = (lane >= start) & (lane < start + SUB)
+        rows[b] = jnp.where(in_block, jnp.where(lane - start == sub, 1.0, 0.0), rows[b])
+        for g in range(b + 1, groups):
+            rows[g] = jnp.where(in_block, 0.0, rows[g])
         pivot = jnp.ones(full, jnp.float32)
         for k in range(0, SUB, 2):
             p, side, q = entry[k, k], entry[k + 1, k], entry[k + 1, k + 1]
@@ -83,60 +92,43 @@
                 reduced = right[m] * inverse
                 for g in range(b, groups):
                     column[m][g] = column[m][g] - first_scale[g] * left[m] - second_scale[g] * reduced
-            ratio = side * inverse
-
-            def lead_of(x):
-                shape = (SUB, x.shape[1])
-                first = jnp.broadcast_to(x[k : k + 1, :], shape)
-                wide = jnp.concatenate([ratio] * (x.shape[1] // LANES), 1)
-                return first, jnp.broadcast_to(x[k + 1 : k + 2, :], shape) - wide * first
-
-            lead = lead_of(rows[b])
-            lead_near = lead_of(near[b])
+            lead = jnp.broadcast_to(rows[b][k : k + 1, :], (SUB, width))
+            next_lead = jnp.broadcast_to(rows[b][k + 1 : k + 2, :], (SUB, width)) - widened(side * inverse) * lead
             for g in range(b, groups):
-                one = jnp.concatenate([first_scale[g]] * (width // LANES), 1)
-                two = jnp.concatenate([second_scale[g]] * (width // LANES), 1)
-                rows[g] = rows[g] - one * lead[0] - two * lead[1]
-                near[g] = near[g] - first_scale[g] * lead_near[0] - second_scale[g] * lead_near[1]
+                rows[g] = rows[g] - widened(first_scale[g]) * lead - widened(second_scale[g]) * next_lead
         pivots[b] = pivot
     return rows, pivots
 
 
 def whiten_kernel(vertex_count, parts_ref, hidden_ref, white_ref, loss_ref, a_ref, v_ref):
     width = a_ref.shape[0]
-    groups = PANEL // SUB
     packed = jnp.concatenate([parts_ref[:width, :], parts_ref[width : 2 * width, :]], 1)
     row, col = iota((width, width), 0), iota((width, width), 1)
     gram = jnp.where(row >= col, packed, packed.T)
     a_ref[...] = gram / vertex_count + jnp.where(row == col, EPSILON, 0.0)
 
-    def panel(j, carry):
-        first = pl.multiple_of(j * PANEL, PANEL)
-        block = a_ref[pl.ds(first, PANEL), :]
-        turned = pltpu.roll(block, lax.rem(width - first, width), 1)[:, :LANES]
+    for first in range(0, width, PANEL):
+        last = first + PANEL
         rows, pivots = eliminate_panel(
-            [block[SUB * g : SUB * g + SUB] for g in range(groups)],
-            [turned[SUB * g : SUB * g + SUB] for g in range(groups)],
-            first,
-            width,
+            [a_ref[i : i + SUB, :] for i in range(first, last, SUB)], first
         )
         whole = jnp.concatenate(rows, 0)
         pivot = jnp.concatenate(pivots, 0)
         pivot = jnp.concatenate([pivot] * (width // LANES), 1)
         lane = iota((PANEL, width), 1)
         lower = lane <= iota((PANEL, width), 0) + first
-        v_ref[pl.ds(first, PANEL), :] = jnp.where(lower, whole * lax.rsqrt(pivot), 0.0)
-        h, m, l = three_terms(whole / pivot)
-        hh, mm, ll = three_terms(jnp.where(lower | (lane >= first + PANEL), whole, 0.0))
+        v_ref[first:last, :] = jnp.where(lower, whole * lax.rsqrt(pivot), 0.0)
+        if last == width:
+            break
+        below = last // LANES * LANES
+        h, m, l = three_terms((whole / pivot)[:, below:])
+        hh, mm, ll = three_terms(jnp.where(lower | (lane >= last), whole, 0.0))
         update = contract(
-            jnp.concatenate([h, h, m, h, l, m], 0), jnp.concatenate([hh, mm, hh, ll, hh, mm], 0), ((0,), (0,))
-        )
-        lanes = iota((width, width), 1)
-        kept = jnp.where((lanes >= first) & (lanes < first + PANEL), 0.0, a_ref[...])
-        a_ref[...] = kept - update
-        return carry
-
-    lax.fori_loop(0, width // PANEL, panel, 0, unroll=True)
+            jnp.concatenate([h, h, m, h], 0), jnp.concatenate([hh, mm, hh, ll], 0), ((0,), (0,))
+        ) + contract(jnp.concatenate([l, m], 0), jnp.concatenate([hh, mm], 0), ((0,), (0,)))
+        lanes = iota((width - below, width), 1)
+        kept = jnp.where((lanes >= first) & (lanes < last), 0.0, a_ref[below:, :])
+        a_ref[below:, :] = kept - update
 
     inverse = v_ref[...]
     high = inverse.astype(jnp.bfloat16)
@@ -290,32 +282,31 @@
 
 
 def layer_kernel(
-    dst_ref, outer_ref, live_ref, features_ref, own_ref, crossed_ref, tile_ref, weight_ref, inner_sum_ref,
-    square_ref, *rest,
+    dst_ref, outer_ref, live_ref, features_ref, own_ref, crossed_ref, tile_ref, weight_ref, inner_sum_ref, square_ref, *rest
 ):
-    *near_refs, hidden_ref, parts_ref, sum_ref, near_ref, far_ref = rest
+    *near_refs, hidden_ref, parts_ref, sum_ref, table_ref = rest
     own, crossed = (
         ref[...].astype(jnp.float32).reshape(-1, SUB, ref.shape[1]) for ref in (own_ref, crossed_ref)
     )
     core = jnp.where(iota(own.shape, 1) >= SUB // 2, 1, 0)
     far = jnp.where(core == lax.axis_index("c"), own, pltpu.roll(crossed, SUB // 2, 1))
-    far_ref[...] = far.reshape(far_ref.shape).astype(far_ref.dtype)
+    far_rows = own_ref.shape[0]
+    table_ref[:far_rows, :] = far.reshape(own_ref.shape).astype(table_ref.dtype)
     peers = len(near_refs)
-    block = near_ref.shape[0] // peers
     for k, ref in enumerate(near_refs):
-        at = lax.rem(lax.axis_index("y") + peers - k, peers)
-        near_ref[pl.ds(pl.multiple_of(at * block, block), block), :] = ref[...]
+        block = ref.shape[0]
+        at = far_rows + lax.rem(lax.axis_index("y") + peers - k, peers) * block
+        table_ref[pl.ds(pl.multiple_of(at, block), block), :] = ref[...]
     slots, tile = outer_ref.shape[0], tile_ref.shape[1]
-    far_tiles = far_ref.shape[0] // tile
     sum_ref[...] = inner_sum_ref[...]
+    products = []
     for k in range(slots):
-        @pl.when((k < live_ref[0, 1]) & (outer_ref[k] < far_tiles))
-        def _(k=k):
-            add_tile(sum_ref, dst_ref, slots + k, tile_ref[slots + k], far_ref, outer_ref[k])
-
-        @pl.when((k < live_ref[0, 1]) & (outer_ref[k] >= far_tiles))
-        def _(k=k):
-            add_tile(sum_ref, dst_ref, slots + k, tile_ref[slots + k], near_ref, outer_ref[k] - far_tiles)
+        source = table_ref[pl.ds(pl.multiple_of(outer_ref[k] * tile, tile), tile), :]
+        product = contract(tile_ref[slots + k], source, ((1,), (0,)))
+        products.append(jnp.where(k < live_ref[0, 1], product, 0.0))
+    for k, product in enumerate(products):
+        to = pl.ds(pl.multiple_of(dst_ref[slots + k] * tile, tile), tile)
+        sum_ref[to, :] += product
 
     projected = contract(sum_ref[...].astype(jnp.bfloat16), weight_ref[...], ((1,), (0,)))
     features = features_ref[...]
@@ -343,8 +334,7 @@
         out_specs=(VMEM, VMEM),
         scratch_shapes=[
             pltpu.VMEM((rows, width), jnp.float32),
-            pltpu.VMEM((near_rows, width), features.dtype),
-            pltpu.VMEM(far.shape, features.dtype),
+            pltpu.VMEM((far.shape[0] + near_rows, width), features.dtype),
         ],
         compiler_params=pltpu.CompilerParams(vmem_limit_bytes=24 * 2**20),
     )(dst, outer, live, features, far, crossed, tiles, weight, *inner, *near)

time: 107 us -> 106 us (level)
  Pallas kernels: 14.9 us -> 12.9 us
  transfers between devices with their start and end apart: 5 -> 5, of which waited for: 3 -> 3; matrix products, arithmetic and copies ran while one was open for 0% -> 0% of each run, Pallas kernels for 2% -> 1%
where the time goes in v5:
time: 106 us; the launch traced here: 105 us
  blocking collectives  48.2 us (45%)
  starting transfers between devices  34.9 us (33%)
  Pallas kernels  12.9 us (12%)
  waiting for transfers between devices  7.76 us (7%)
    all_to_all x1, starting transfers between devices, body(): lax.all_to_all(far.reshape(-1, SUB, width), ('x', 'z'), 0, 0, tiled=True)  19.1 us
    all_to_all x1, blocking collectives, sum_over_all(): own = jnp.sum(lax.all_to_all(own, far, 0, 0, tiled=True), 0)  16.2 us
    all_to_all x1, blocking collectives, sum_over_all(): own = jnp.sum(lax.all_to_all(pieces, near, 0, 0, tiled=True), 0)  16.2 us
    all_to_all x1, blocking collectives, sum_over_all(): return lax.all_to_all(own, near, 0, 0, tiled=True).reshape(parts.shape)  15.8 us
    ppermute x3, starting transfers between devices, body(): lax.ppermute(near[k], 'y', [(i, (i + k) % peers) for i in range(peers)])  11 us
    pallas_call x1, Pallas kernels, whiten(): pl.pallas_call(functools.partial(whiten_kernel, vertex_count), out_shape=...  7.41 us
    all_to_all x1, waiting for transfers between devices, body(): lax.all_to_all(far.reshape(-1, SUB, width), ('x', 'z'), 0, 0, tiled=True)  5.99 us
    ppermute x1, starting transfers between devices, body(): crossed = lax.ppermute(far, 'c', [(0, 1), (1, 0)])  4.78 us
  transfers between devices with their start and end apart: 5, of which 3 were waited for; matrix products, arithmetic and copies ran while one was open for 0% of the time, Pallas kernels for 1%

profile of v5, /device:TPU:1, one launch (start us, length us, event | category | flops | bytes accessed | tf_op | source)
XLA Modules:
  0.0 105.2 jit_solution(14339490863227528103)
XLA Ops:
  0.6 0.0 copy-start
  0.6 0.0 copy-start.1
  0.7 2.4 %shard_map.104 = (bf16[512,256]{1,0:T(8,128)(2,1)}, bf16[32,256]{1,0:T(8,128)(2,1)}, bf16[32,256]{1,0:T(8,128)(2,1)}, bf16[32,256]{1,0:T(8,128)(2,1)}, bf16[32,256]{1,0:T(8,128)(2,1)}) custom-call(bf16[1024,256]{1,0:T(8,128)(2,1)} %features_ref.3, s32[4,128]{1,0:T(4,128)} %bitcast.12, s32[1,128]{1,0:T(1,128)} %bitcast.13), custom_call_target="tpu_custom_call" | custom-call | tf_op jit(solution)/shard_map/pallas_call | solution.py:231
  3.1 19.1 %all-to-all-start = ((bf16[64,8,256]{2,1,0:T(8,128)(2,1)}), bf16[64,8,256]{2,1,0:T(8,128)(2,1)S(1)}, u32[]{:S(2)}, u32[]{:S(2)}) async-start(bf16[64,8,256]{2,1,0:T(8,128)(2,1)} %bitcast.11), calls=%async_computation | async-start | bytes 524288 | tf_op jit(solution)/shard_map/all_to_all | solution.py:359
  22.2 3.2 %collective-permute-start = (bf16[32,256]{1,0:T(8,128)(2,1)}, bf16[32,256]{1,0:T(8,128)(2,1)S(1)}, u32[]{:S(2)}, u32[]{:S(2)}) collective-permute-start(bf16[32,256]{1,0:T(8,128)(2,1)} %get-tuple-element.22), channel_id=1, source_target_pairs={{0,1},{1,2},{2,3},{3,0},{4,5},{5,6},{6,7},{7,4},{8,9},{9,10},{10,1... | collective-permute-start | bytes 49160 | tf_op jit(solution)/shard_map/ppermute | solution.py:361
  25.4 0.0 copy-start.7
  25.4 0.0 copy-start.4
  25.4 0.0 copy-start.5
  25.4 0.0 copy-start.6
  25.5 4.7 %collective-permute-start.1 = (bf16[32,256]{1,0:T(8,128)(2,1)}, bf16[32,256]{1,0:T(8,128)(2,1)S(1)}, u32[]{:S(2)}, u32[]{:S(2)}) collective-permute-start(bf16[32,256]{1,0:T(8,128)(2,1)} %get-tuple-element.23), channel_id=1, source_target_pairs={{0,2},{1,3},{2,0},{3,1},{4,6},{5,7},{6,4},{7,5},{8,10},{9,11},{10,... | collective-permute-start | bytes 49160 | tf_op jit(solution)/shard_map/ppermute | solution.py:361
  30.1 0.0 copy-start.2
  30.1 3.1 %collective-permute-start.2 = (bf16[32,256]{1,0:T(8,128)(2,1)}, bf16[32,256]{1,0:T(8,128)(2,1)S(1)}, u32[]{:S(2)}, u32[]{:S(2)}) collective-permute-start(bf16[32,256]{1,0:T(8,128)(2,1)} %get-tuple-element.24), channel_id=1, source_target_pairs={{0,3},{1,0},{2,1},{3,2},{4,7},{5,4},{6,5},{7,6},{8,11},{9,8},{10,9... | collective-permute-start | bytes 49160 | tf_op jit(solution)/shard_map/ppermute | solution.py:361
  33.2 0.0 copy-done
  33.3 0.0 copy-done.1
  33.3 0.0 copy-done.7
  33.3 0.0 copy-done.4
  33.3 1.3 %shard_map.105 = (f32[1024,256]{1,0:T(8,128)S(1)}, f32[8,128]{1,0:T(8,128)S(1)}) custom-call(s32[16]{0:T(128)S(1)} %copy-done.4, s32[8]{0:T(128)S(1)} %copy-done.7, s32[8]{0:T(128)S(1)} %copy-done.5, s32[1,2]{1,0:T(1,128)S(1)} %copy-done.6, bf16[1024,256]{1,0:T(8,128)(2,1)S(1)} %copy-done, bf16[16,128,128]{2,1,0:T(8,128)(2,1)S(1)} %copy-done.1), custom_call_target="tpu_custom_call" | custom-call | flops 100000000 | bytes 2000000 | tf_op jit(solution)/shard_map/pallas_call | solution.py:271
  34.6 0.0 collective-permute-done.rest_1_
  34.6 0.0 collective-permute-done.1.rest_2_
  34.6 0.6 collective-permute-done.2.rest_3_
  35.3 6.0 %all-to-all-done = bf16[64,8,256]{2,1,0:T(8,128)(2,1)S(1)} async-done(((bf16[64,8,256]{2,1,0:T(8,128)(2,1)}), bf16[64,8,256]{2,1,0:T(8,128)(2,1)S(1)}, u32[]{:S(2)}, u32[]{:S(2)}) %all-to-all-start) | async-done | bytes 262176 | tf_op jit(solution)/shard_map/all_to_all | solution.py:359
  41.2 4.8 %collective-permute-start.3 = (bf16[512,256]{1,0:T(8,128)(2,1)S(1)}, bf16[512,256]{1,0:T(8,128)(2,1)S(1)}, u32[]{:S(2)}, u32[]{:S(2)}) collective-permute-start(bf16[512,256]{1,0:T(8,128)(2,1)S(1)} %bitcast.8), channel_id=1, source_target_pairs={{0,4},{4,0},{1,5},{5,1},{2,6},{6,2},{3,7},{7,3},{8,12},{12,8},{9,1... | collective-permute-start | bytes 786440 | tf_op jit(solution)/shard_map/ppermute | solution.py:365
  46.0 1.1 %collective-permute-done.3.crossed_ref = bf16[512,256]{1,0:T(8,128)(2,1)S(1)} collective-permute-done((bf16[512,256]{1,0:T(8,128)(2,1)S(1)}, bf16[512,256]{1,0:T(8,128)(2,1)S(1)}, u32[]{:S(2)}, u32[]{:S(2)}) %collective-permute-start.3) | collective-permute-done | bytes 262176 | tf_op jit(solution)/shard_map/ppermute | solution.py:365
  47.2 1.8 %shard_map.106 = (bf16[1024,256]{1,0:T(8,128)(2,1)S(1)}, f32[544,128]{1,0:T(8,128)S(1)}) custom-call(s32[16]{0:T(128)S(1)} %copy-done.4, s32[8]{0:T(128)S(1)} %copy-done.5, s32[1,2]{1,0:T(1,128)S(1)} %copy-done.6, bf16[1024,256]{1,0:T(8,128)(2,1)S(1)} %copy-done, bf16[512,256]{1,0:T(8,128)(2,1)S(1)} %bitcast.9, ...), custom_call_target="tpu_custom_call" | custom-call | tf_op jit(solution)/shard_map/pallas_call | solution.py:327
  49.0 16.2 %all_to_all.20 = f32[32,1,2176]{2,1,0:T(1,128)S(1)} all-to-all(f32[32,1,2176]{2,1,0:T(1,128)S(1)} %bitcast.10), channel_id=1, replica_groups=mesh['x'=4,'z'=16,'c'=2,'y'=4] {'x','c','y'}, dimensions={0} | all-to-all | bytes 557056 | tf_op jit(solution)/shard_map/all_to_all | solution.py:346
  65.2 0.2 reduce_sum.18
  65.4 0.1 broadcast_in_dim.4
  65.5 16.2 %all_to_all.21 = f32[16,1,2176]{2,1,0:T(1,128)S(1)} all-to-all(f32[16,1,2176]{2,1,0:T(1,128)S(1)} %broadcast_in_dim.4), channel_id=1, replica_groups=mesh['x'=4,'z'=16,'c'=2,'y'=4] {'z'}, dimensions={0} | all-to-all | bytes 278528 | tf_op jit(solution)/shard_map/all_to_all | solution.py:348
  81.7 0.1 reduce_sum.19
  81.8 0.1 broadcast_in_dim.5
  81.9 15.8 %all_to_all.22 = f32[32,1,2176]{2,1,0:T(1,128)S(1)} all-to-all(f32[32,1,2176]{2,1,0:T(1,128)S(1)} %broadcast_in_dim.5), channel_id=1, replica_groups=mesh['x'=4,'z'=16,'c'=2,'y'=4] {'x','c','y'}, dimensions={0} | all-to-all | bytes 557056 | tf_op jit(solution)/shard_map/all_to_all | solution.py:350
  97.8 7.4 %shard_map.107 = (bf16[1024,256]{1,0:T(8,128)(2,1)}, f32[1,1]{1,0:T(1,128)}) custom-call(f32[544,128]{1,0:T(8,128)S(1)} %bitcast.7, bf16[1024,256]{1,0:T(8,128)(2,1)S(1)} %get-tuple-element.35.hidden_ref), custom_call_target="tpu_custom_call" | custom-call | tf_op jit(solution)/shard_map/pallas_call | solution.py:154
  (5 shorter events, 0.0 us)
Async XLA Ops:
  0.6 32.6 %copy-start = (bf16[1024,256]{1,0:T(8,128)(2,1)S(1)}, bf16[1024,256]{1,0:T(8,128)(2,1)}, u32[]{:S(2)}) copy-start(bf16[1024,256]{1,0:T(8,128)(2,1)} %features_ref.3) | copy-start | bytes 1572868
  0.6 32.6 %copy-start.1 = (bf16[16,128,128]{2,1,0:T(8,128)(2,1)S(1)}, bf16[16,128,128]{2,1,0:T(8,128)(2,1)}, u32[]{:S(2)}) copy-start(bf16[16,128,128]{2,1,0:T(8,128)(2,1)} %tile_ref.3) | copy-start | bytes 1572868
  3.1 38.2 %all-to-all-start = ((bf16[64,8,256]{2,1,0:T(8,128)(2,1)}), bf16[64,8,256]{2,1,0:T(8,128)(2,1)S(1)}, u32[]{:S(2)}, u32[]{:S(2)}) async-start(bf16[64,8,256]{2,1,0:T(8,128)(2,1)} %bitcast.11), calls=%async_computation | async-start | bytes 524288 | tf_op jit(solution)/shard_map/all_to_all | solution.py:359
  22.2 12.4 %collective-permute-start = (bf16[32,256]{1,0:T(8,128)(2,1)}, bf16[32,256]{1,0:T(8,128)(2,1)S(1)}, u32[]{:S(2)}, u32[]{:S(2)}) collective-permute-start(bf16[32,256]{1,0:T(8,128)(2,1)} %get-tuple-element.22), channel_id=1, source_target_pairs={{0,1},{1,2},{2,3},{3,0},{4,5},{5,6},{6,7},{7,4},{8,9},{9,10},{10,1... | collective-permute-start | bytes 49160 | tf_op jit(solution)/shard_map/ppermute | solution.py:361
  25.4 7.9 %copy-start.7 = (s32[8]{0:T(128)S(1)}, s32[8]{0:T(128)}, u32[]{:S(2)}) copy-start(s32[8]{0:T(128)} %inner_ref.1) | copy-start | bytes 100
  25.4 7.9 %copy-start.4 = (s32[16]{0:T(128)S(1)}, s32[16]{0:T(128)}, u32[]{:S(2)}) copy-start(s32[16]{0:T(128)} %dst_ref.3) | copy-start | bytes 196
  25.4 7.9 %copy-start.5 = (s32[8]{0:T(128)S(1)}, s32[8]{0:T(128)}, u32[]{:S(2)}) copy-start(s32[8]{0:T(128)} %outer_ref.3) | copy-start | bytes 100
  25.4 7.9 %copy-start.6 = (s32[1,2]{1,0:T(1,128)S(1)}, s32[1,2]{1,0:T(1,128)}, u32[]{:S(2)}) copy-start(s32[1,2]{1,0:T(1,128)} %live_ref.3) | copy-start | bytes 28
  25.5 9.2 %collective-permute-start.1 = (bf16[32,256]{1,0:T(8,128)(2,1)}, bf16[32,256]{1,0:T(8,128)(2,1)S(1)}, u32[]{:S(2)}, u32[]{:S(2)}) collective-permute-start(bf16[32,256]{1,0:T(8,128)(2,1)} %get-tuple-element.23), channel_id=1, source_target_pairs={{0,2},{1,3},{2,0},{3,1},{4,6},{5,7},{6,4},{7,5},{8,10},{9,11},{10,... | collective-permute-start | bytes 49160 | tf_op jit(solution)/shard_map/ppermute | solution.py:361
  30.1 17.1 %copy-start.2 = (bf16[256,256]{1,0:T(8,128)(2,1)S(1)}, bf16[256,256]{1,0:T(8,128)(2,1)}, u32[]{:S(2)}) copy-start(bf16[256,256]{1,0:T(8,128)(2,1)} %weight_ref.1) | copy-start | bytes 393220
  30.1 5.1 %collective-permute-start.2 = (bf16[32,256]{1,0:T(8,128)(2,1)}, bf16[32,256]{1,0:T(8,128)(2,1)S(1)}, u32[]{:S(2)}, u32[]{:S(2)}) collective-permute-start(bf16[32,256]{1,0:T(8,128)(2,1)} %get-tuple-element.24), channel_id=1, source_target_pairs={{0,3},{1,0},{2,1},{3,2},{4,7},{5,4},{6,5},{7,6},{8,11},{9,8},{10,9... | collective-permute-start | bytes 49160 | tf_op jit(solution)/shard_map/ppermute | solution.py:361
  33.3 13.9 %copy-start.3 = (bf16[32,256]{1,0:T(8,128)(2,1)S(1)}, bf16[32,256]{1,0:T(8,128)(2,1)}, u32[]{:S(2)}) copy-start(bf16[32,256]{1,0:T(8,128)(2,1)} %get-tuple-element.30.rest_0_) | copy-start | bytes 49156
  41.2 5.9 %collective-permute-start.3 = (bf16[512,256]{1,0:T(8,128)(2,1)S(1)}, bf16[512,256]{1,0:T(8,128)(2,1)S(1)}, u32[]{:S(2)}, u32[]{:S(2)}) collective-permute-start(bf16[512,256]{1,0:T(8,128)(2,1)S(1)} %bitcast.8), channel_id=1, source_target_pairs={{0,4},{4,0},{1,5},{5,1},{2,6},{6,2},{3,7},{7,3},{8,12},{12,8},{9,1... | collective-permute-start | bytes 786440 | tf_op jit(solution)/shard_map/ppermute | solution.py:365

commit v6 on v5

--- a/solution.py
+++ b/solution.py
@@ -49,10 +49,10 @@
     def widened(x):
         return jnp.concatenate([x] * (width // LANES), 1)
 
-    for b in range(groups):
+    def columns_of(b):
         start = first_lane + SUB * b
         part = slice(start // LANES * LANES, start // LANES * LANES + LANES)
-        column = [
+        return [
             {
                 g: jnp.take_along_axis(
                     rows[g][:, part], jnp.full(full, start % LANES + k, jnp.int32), 1, mode="promise_in_bounds"
@@ -61,6 +61,12 @@
             }
             for k in range(SUB)
         ]
+
+    ahead = []
+    for b in range(groups):
+        start = first_lane + SUB * b
+        column = ahead if ahead else columns_of(b)
+        ahead = columns_of(b + 1) if 0 < groups - b - 1 <= 3 else []
         entry = {
             (m, k): jnp.broadcast_to(column[k][b][m : m + 1, :], full) for k in range(SUB) for m in range(k, SUB)
         }
@@ -84,8 +90,16 @@
             first_scale, second_scale = {}, {}
             for g in range(b, groups):
                 x, y = column[k][g], column[k + 1][g]
+                below = p * y - side * x
                 first_scale[g] = x * inverse
-                second_scale[g] = (p * y - side * x) * second
+                second_scale[g] = below * second
+                if ahead and g == b + 1:
+                    next_left, next_right = x, below * inverse
+            for m in range(SUB if ahead else 0):
+                one = jnp.broadcast_to(next_left[m : m + 1, :], full)
+                two = jnp.broadcast_to(next_right[m : m + 1, :], full)
+                for g in range(b + 1, groups):
+                    ahead[m][g] = ahead[m][g] - first_scale[g] * one - second_scale[g] * two
             first_scale[b] = jnp.where(sub_lane > k, first_scale[b], 0.0)
             second_scale[b] = jnp.where(sub_lane > k + 1, second_scale[b], 0.0)
             for m in range(k + 2, SUB):

time: 106 us -> 106 us (level)
  transfers between devices with their start and end apart: 5 -> 5, of which waited for: 3 -> 2; matrix products, arithmetic and copies ran while one was open for 0% -> 0% of each run, Pallas kernels for 1% -> 2%
where the time goes in v6:
time: 106 us; the launch traced here: 105 us
  blocking collectives  48.2 us (45%)
  starting transfers between devices  34.9 us (33%)
  Pallas kernels  13.4 us (13%)
  waiting for transfers between devices  7.19 us (7%)
    all_to_all x1, starting transfers between devices, body(): lax.all_to_all(far.reshape(-1, SUB, width), ('x', 'z'), 0, 0, tiled=True)  19.1 us
    all_to_all x1, blocking collectives, sum_over_all(): own = jnp.sum(lax.all_to_all(own, far, 0, 0, tiled=True), 0)  16.2 us
    all_to_all x1, blocking collectives, sum_over_all(): own = jnp.sum(lax.all_to_all(pieces, near, 0, 0, tiled=True), 0)  16.2 us
    all_to_all x1, blocking collectives, sum_over_all(): return lax.all_to_all(own, near, 0, 0, tiled=True).reshape(parts.shape)  15.8 us
    ppermute x3, starting transfers between devices, body(): lax.ppermute(near[k], 'y', [(i, (i + k) % peers) for i in range(peers)])  11 us
    pallas_call x1, Pallas kernels, whiten(): pl.pallas_call(functools.partial(whiten_kernel, vertex_count), out_shape=...  7.33 us
    all_to_all x1, waiting for transfers between devices, body(): lax.all_to_all(far.reshape(-1, SUB, width), ('x', 'z'), 0, 0, tiled=True)  5.99 us
    ppermute x1, starting transfers between devices, body(): crossed = lax.ppermute(far, 'c', [(0, 1), (1, 0)])  4.78 us
  transfers between devices with their start and end apart: 5, of which 2 were waited for; matrix products, arithmetic and copies ran while one was open for 0% of the time, Pallas kernels for 2%

profile of v6, /device:TPU:1, one launch (start us, length us, event | category | flops | bytes accessed | tf_op | source)
XLA Modules:
  0.0 105.1 jit_solution(10549723437388615940)
XLA Ops:
  0.6 0.0 copy-start
  0.6 0.0 copy-start.1
  0.7 2.4 %shard_map.104 = (bf16[512,256]{1,0:T(8,128)(2,1)}, bf16[32,256]{1,0:T(8,128)(2,1)}, bf16[32,256]{1,0:T(8,128)(2,1)}, bf16[32,256]{1,0:T(8,128)(2,1)}, bf16[32,256]{1,0:T(8,128)(2,1)}) custom-call(bf16[1024,256]{1,0:T(8,128)(2,1)} %features_ref.3, s32[4,128]{1,0:T(4,128)} %bitcast.12, s32[1,128]{1,0:T(1,128)} %bitcast.13), custom_call_target="tpu_custom_call" | custom-call | tf_op jit(solution)/shard_map/pallas_call | solution.py:245
  3.1 19.1 %all-to-all-start = ((bf16[64,8,256]{2,1,0:T(8,128)(2,1)}), bf16[64,8,256]{2,1,0:T(8,128)(2,1)S(1)}, u32[]{:S(2)}, u32[]{:S(2)}) async-start(bf16[64,8,256]{2,1,0:T(8,128)(2,1)} %bitcast.11), calls=%async_computation | async-start | bytes 524288 | tf_op jit(solution)/shard_map/all_to_all | solution.py:373
  22.2 3.2 %collective-permute-start = (bf16[32,256]{1,0:T(8,128)(2,1)}, bf16[32,256]{1,0:T(8,128)(2,1)S(1)}, u32[]{:S(2)}, u32[]{:S(2)}) collective-permute-start(bf16[32,256]{1,0:T(8,128)(2,1)} %get-tuple-element.22), channel_id=1, source_target_pairs={{0,1},{1,2},{2,3},{3,0},{4,5},{5,6},{6,7},{7,4},{8,9},{9,10},{10,1... | collective-permute-start | bytes 49160 | tf_op jit(solution)/shard_map/ppermute | solution.py:375
  25.4 0.0 copy-start.7
  25.4 0.0 copy-start.4
  25.4 0.0 copy-start.5
  25.4 0.0 copy-start.6
  25.5 4.7 %collective-permute-start.1 = (bf16[32,256]{1,0:T(8,128)(2,1)}, bf16[32,256]{1,0:T(8,128)(2,1)S(1)}, u32[]{:S(2)}, u32[]{:S(2)}) collective-permute-start(bf16[32,256]{1,0:T(8,128)(2,1)} %get-tuple-element.23), channel_id=1, source_target_pairs={{0,2},{1,3},{2,0},{3,1},{4,6},{5,7},{6,4},{7,5},{8,10},{9,11},{10,... | collective-permute-start | bytes 49160 | tf_op jit(solution)/shard_map/ppermute | solution.py:375
  30.1 0.0 copy-start.2
  30.1 3.1 %collective-permute-start.2 = (bf16[32,256]{1,0:T(8,128)(2,1)}, bf16[32,256]{1,0:T(8,128)(2,1)S(1)}, u32[]{:S(2)}, u32[]{:S(2)}) collective-permute-start(bf16[32,256]{1,0:T(8,128)(2,1)} %get-tuple-element.24), channel_id=1, source_target_pairs={{0,3},{1,0},{2,1},{3,2},{4,7},{5,4},{6,5},{7,6},{8,11},{9,8},{10,9... | collective-permute-start | bytes 49160 | tf_op jit(solution)/shard_map/ppermute | solution.py:375
  33.2 0.0 copy-done
  33.3 0.0 copy-done.1
  33.3 0.0 copy-done.7
  33.3 1.9 %shard_map.105 = (f32[1024,256]{1,0:T(8,128)S(1)}, f32[8,128]{1,0:T(8,128)S(1)}) custom-call(s32[16]{0:T(128)S(1)} %copy-done.4, s32[8]{0:T(128)S(1)} %copy-done.7, s32[8]{0:T(128)S(1)} %copy-done.5, s32[1,2]{1,0:T(1,128)S(1)} %copy-done.6, bf16[1024,256]{1,0:T(8,128)(2,1)S(1)} %copy-done, bf16[16,128,128]{2,1,0:T(8,128)(2,1)S(1)} %copy-done.1), custom_call_target="tpu_custom_call" | custom-call | flops 100000000 | bytes 2000000 | tf_op jit(solution)/shard_map/pallas_call | solution.py:285
  35.2 0.0 collective-permute-done.rest_1_
  35.2 0.0 collective-permute-done.1.rest_2_
  35.2 0.0 collective-permute-done.2.rest_3_
  35.3 6.0 %all-to-all-done = bf16[64,8,256]{2,1,0:T(8,128)(2,1)S(1)} async-done(((bf16[64,8,256]{2,1,0:T(8,128)(2,1)}), bf16[64,8,256]{2,1,0:T(8,128)(2,1)S(1)}, u32[]{:S(2)}, u32[]{:S(2)}) %all-to-all-start) | async-done | bytes 262176 | tf_op jit(solution)/shard_map/all_to_all | solution.py:373
  41.2 4.8 %collective-permute-start.3 = (bf16[512,256]{1,0:T(8,128)(2,1)S(1)}, bf16[512,256]{1,0:T(8,128)(2,1)S(1)}, u32[]{:S(2)}, u32[]{:S(2)}) collective-permute-start(bf16[512,256]{1,0:T(8,128)(2,1)S(1)} %bitcast.8), channel_id=1, source_target_pairs={{0,4},{4,0},{1,5},{5,1},{2,6},{6,2},{3,7},{7,3},{8,12},{12,8},{9,1... | collective-permute-start | bytes 786440 | tf_op jit(solution)/shard_map/ppermute | solution.py:379
  46.0 1.1 %collective-permute-done.3.crossed_ref = bf16[512,256]{1,0:T(8,128)(2,1)S(1)} collective-permute-done((bf16[512,256]{1,0:T(8,128)(2,1)S(1)}, bf16[512,256]{1,0:T(8,128)(2,1)S(1)}, u32[]{:S(2)}, u32[]{:S(2)}) %collective-permute-start.3) | collective-permute-done | bytes 262176 | tf_op jit(solution)/shard_map/ppermute | solution.py:379
  47.2 0.0 copy-done.3
  47.2 1.8 %shard_map.106 = (bf16[1024,256]{1,0:T(8,128)(2,1)S(1)}, f32[544,128]{1,0:T(8,128)S(1)}) custom-call(s32[16]{0:T(128)S(1)} %copy-done.4, s32[8]{0:T(128)S(1)} %copy-done.5, s32[1,2]{1,0:T(1,128)S(1)} %copy-done.6, bf16[1024,256]{1,0:T(8,128)(2,1)S(1)} %copy-done, bf16[512,256]{1,0:T(8,128)(2,1)S(1)} %bitcast.9, ...), custom_call_target="tpu_custom_call" | custom-call | tf_op jit(solution)/shard_map/pallas_call | solution.py:341
  49.0 16.2 %all_to_all.20 = f32[32,1,2176]{2,1,0:T(1,128)S(1)} all-to-all(f32[32,1,2176]{2,1,0:T(1,128)S(1)} %bitcast.10), channel_id=1, replica_groups=mesh['x'=4,'z'=16,'c'=2,'y'=4] {'x','c','y'}, dimensions={0} | all-to-all | bytes 557056 | tf_op jit(solution)/shard_map/all_to_all | solution.py:360
  65.2 0.2 reduce_sum.18
  65.4 0.1 broadcast_in_dim.4
  65.5 16.2 %all_to_all.21 = f32[16,1,2176]{2,1,0:T(1,128)S(1)} all-to-all(f32[16,1,2176]{2,1,0:T(1,128)S(1)} %broadcast_in_dim.4), channel_id=1, replica_groups=mesh['x'=4,'z'=16,'c'=2,'y'=4] {'z'}, dimensions={0} | all-to-all | bytes 278528 | tf_op jit(solution)/shard_map/all_to_all | solution.py:362
  81.7 0.1 reduce_sum.19
  81.8 0.1 broadcast_in_dim.5
  81.9 15.8 %all_to_all.22 = f32[32,1,2176]{2,1,0:T(1,128)S(1)} all-to-all(f32[32,1,2176]{2,1,0:T(1,128)S(1)} %broadcast_in_dim.5), channel_id=1, replica_groups=mesh['x'=4,'z'=16,'c'=2,'y'=4] {'x','c','y'}, dimensions={0} | all-to-all | bytes 557056 | tf_op jit(solution)/shard_map/all_to_all | solution.py:364
  97.8 7.3 %shard_map.107 = (bf16[1024,256]{1,0:T(8,128)(2,1)}, f32[1,1]{1,0:T(1,128)}) custom-call(f32[544,128]{1,0:T(8,128)S(1)} %bitcast.7, bf16[1024,256]{1,0:T(8,128)(2,1)S(1)} %get-tuple-element.35.hidden_ref), custom_call_target="tpu_custom_call" | custom-call | tf_op jit(solution)/shard_map/pallas_call | solution.py:168
  (5 shorter events, 0.0 us)
Async XLA Ops:
  0.6 32.6 %copy-start = (bf16[1024,256]{1,0:T(8,128)(2,1)S(1)}, bf16[1024,256]{1,0:T(8,128)(2,1)}, u32[]{:S(2)}) copy-start(bf16[1024,256]{1,0:T(8,128)(2,1)} %features_ref.3) | copy-start | bytes 1572868
  0.6 32.6 %copy-start.1 = (bf16[16,128,128]{2,1,0:T(8,128)(2,1)S(1)}, bf16[16,128,128]{2,1,0:T(8,128)(2,1)}, u32[]{:S(2)}) copy-start(bf16[16,128,128]{2,1,0:T(8,128)(2,1)} %tile_ref.3) | copy-start | bytes 1572868
  3.1 38.2 %all-to-all-start = ((bf16[64,8,256]{2,1,0:T(8,128)(2,1)}), bf16[64,8,256]{2,1,0:T(8,128)(2,1)S(1)}, u32[]{:S(2)}, u32[]{:S(2)}) async-start(bf16[64,8,256]{2,1,0:T(8,128)(2,1)} %bitcast.11), calls=%async_computation | async-start | bytes 524288 | tf_op jit(solution)/shard_map/all_to_all | solution.py:373
  22.2 13.0 %collective-permute-start = (bf16[32,256]{1,0:T(8,128)(2,1)}, bf16[32,256]{1,0:T(8,128)(2,1)S(1)}, u32[]{:S(2)}, u32[]{:S(2)}) collective-permute-start(bf16[32,256]{1,0:T(8,128)(2,1)} %get-tuple-element.22), channel_id=1, source_target_pairs={{0,1},{1,2},{2,3},{3,0},{4,5},{5,6},{6,7},{7,4},{8,9},{9,10},{10,1... | collective-permute-start | bytes 49160 | tf_op jit(solution)/shard_map/ppermute | solution.py:375
  25.4 7.9 %copy-start.7 = (s32[8]{0:T(128)S(1)}, s32[8]{0:T(128)}, u32[]{:S(2)}) copy-start(s32[8]{0:T(128)} %inner_ref.1) | copy-start | bytes 100
  25.4 7.9 %copy-start.4 = (s32[16]{0:T(128)S(1)}, s32[16]{0:T(128)}, u32[]{:S(2)}) copy-start(s32[16]{0:T(128)} %dst_ref.3) | copy-start | bytes 196
  25.4 7.9 %copy-start.5 = (s32[8]{0:T(128)S(1)}, s32[8]{0:T(128)}, u32[]{:S(2)}) copy-start(s32[8]{0:T(128)} %outer_ref.3) | copy-start | bytes 100
  25.4 7.9 %copy-start.6 = (s32[1,2]{1,0:T(1,128)S(1)}, s32[1,2]{1,0:T(1,128)}, u32[]{:S(2)}) copy-start(s32[1,2]{1,0:T(1,128)} %live_ref.3) | copy-start | bytes 28
  25.5 9.7 %collective-permute-start.1 = (bf16[32,256]{1,0:T(8,128)(2,1)}, bf16[32,256]{1,0:T(8,128)(2,1)S(1)}, u32[]{:S(2)}, u32[]{:S(2)}) collective-permute-start(bf16[32,256]{1,0:T(8,128)(2,1)} %get-tuple-element.23), channel_id=1, source_target_pairs={{0,2},{1,3},{2,0},{3,1},{4,6},{5,7},{6,4},{7,5},{8,10},{9,11},{10,... | collective-permute-start | bytes 49160 | tf_op jit(solution)/shard_map/ppermute | solution.py:375
  30.1 17.1 %copy-start.2 = (bf16[256,256]{1,0:T(8,128)(2,1)S(1)}, bf16[256,256]{1,0:T(8,128)(2,1)}, u32[]{:S(2)}) copy-start(bf16[256,256]{1,0:T(8,128)(2,1)} %weight_ref.1) | copy-start | bytes 393220
  30.1 5.1 %collective-permute-start.2 = (bf16[32,256]{1,0:T(8,128)(2,1)}, bf16[32,256]{1,0:T(8,128)(2,1)S(1)}, u32[]{:S(2)}, u32[]{:S(2)}) collective-permute-start(bf16[32,256]{1,0:T(8,128)(2,1)} %get-tuple-element.24), channel_id=1, source_target_pairs={{0,3},{1,0},{2,1},{3,2},{4,7},{5,4},{6,5},{7,6},{8,11},{9,8},{10,9... | collective-permute-start | bytes 49160 | tf_op jit(solution)/shard_map/ppermute | solution.py:375
  33.3 13.9 %copy-start.3 = (bf16[32,256]{1,0:T(8,128)(2,1)S(1)}, bf16[32,256]{1,0:T(8,128)(2,1)}, u32[]{:S(2)}) copy-start(bf16[32,256]{1,0:T(8,128)(2,1)} %get-tuple-element.30.rest_0_) | copy-start | bytes 49156
  41.2 5.9 %collective-permute-start.3 = (bf16[512,256]{1,0:T(8,128)(2,1)S(1)}, bf16[512,256]{1,0:T(8,128)(2,1)S(1)}, u32[]{:S(2)}, u32[]{:S(2)}) collective-permute-start(bf16[512,256]{1,0:T(8,128)(2,1)S(1)} %bitcast.8), channel_id=1, source_target_pairs={{0,4},{4,0},{1,5},{5,1},{2,6},{6,2},{3,7},{7,3},{8,12},{12,8},{9,1... | collective-permute-start | bytes 786440 | tf_op jit(solution)/shard_map/ppermute | solution.py:379

commit v7 on v5

--- a/solution.py
+++ b/solution.py
@@ -357,9 +357,11 @@
     peers = lax.axis_size("y")
     far, *near = gather(features, send_far, send_near, peers)
     far = lax.all_to_all(far.reshape(-1, SUB, width), ("x", "z"), 0, 0, tiled=True).reshape(-1, width)
-    near = near[:1] + [
-        lax.ppermute(near[k], "y", [(i, (i + k) % peers) for i in range(peers)]) for k in range(1, peers)
-    ]
+    by_one, by_two = ([(i, (i + k) % peers) for i in range(peers)] for k in (1, 2))
+    block = near[0].shape[0]
+    first = lax.ppermute(jnp.concatenate([near[1], near[3]]), "y", by_one)
+    second = lax.ppermute(jnp.concatenate([near[2], first[block:]]), "y", by_two)
+    near = [near[0], first[:block], second[:block], second[block:]]
     inner = inner_sums(tile_dst, inner_src, outer_src, tile_live, features, tile_weight)
     far, near, inner = lax.optimization_barrier((far, near, inner))
     crossed = lax.ppermute(far, "c", [(0, 1), (1, 0)])

time: 106 us -> 106 us (level)
  starting transfers between devices: 34.9 us -> 30.8 us
  waiting for transfers between devices: 7.76 us -> 10.9 us
    ppermute x3 -> x2, starting transfers between devices: 11 us -> 6.87 us  [the longest x1 3.54 us: body(): lax.ppermute(jnp.concatenate([near[2], first[block:]]), 'y', by_two)]
    ppermute x3 -> x2, waiting for transfers between devices: 0.63 us -> 4.28 us  [the longest x1 3.02 us: body(): first = lax.ppermute(jnp.concatenate([near[1], near[3]]), 'y', by_one)]
  transfers between devices with their start and end apart: 5 -> 4, of which waited for: 3 -> 4; matrix products, arithmetic and copies ran while one was open for 0% -> 1% of each run, Pallas kernels for 1% -> 1%
where the time goes in v7:
time: 106 us; the launch traced here: 105 us
  blocking collectives  48.5 us (46%)
  starting transfers between devices  30.8 us (29%)
  Pallas kernels  13.2 us (12%)
  waiting for transfers between devices  10.9 us (10%)
    all_to_all x1, starting transfers between devices, body(): lax.all_to_all(far.reshape(-1, SUB, width), ('x', 'z'), 0, 0, tiled=True)  19.1 us
    all_to_all x1, blocking collectives, sum_over_all(): own = jnp.sum(lax.all_to_all(own, far, 0, 0, tiled=True), 0)  16.4 us
    all_to_all x1, blocking collectives, sum_over_all(): own = jnp.sum(lax.all_to_all(pieces, near, 0, 0, tiled=True), 0)  16.2 us
    all_to_all x1, blocking collectives, sum_over_all(): return lax.all_to_all(own, near, 0, 0, tiled=True).reshape(parts.shape)  15.8 us
    pallas_call x1, Pallas kernels, whiten(): pl.pallas_call(functools.partial(whiten_kernel, vertex_count), out_shape=...  7.4 us
    all_to_all x1, waiting for transfers between devices, body(): lax.all_to_all(far.reshape(-1, SUB, width), ('x', 'z'), 0, 0, tiled=True)  5.43 us
    ppermute x1, starting transfers between devices, body(): crossed = lax.ppermute(far, 'c', [(0, 1), (1, 0)])  4.78 us
    ppermute x1, starting transfers between devices, body(): lax.ppermute(jnp.concatenate([near[2], first[block:]]), 'y', by_two)  3.54 us
  transfers between devices with their start and end apart: 4, of which 4 were waited for; matrix products, arithmetic and copies ran while one was open for 1% of the time, Pallas kernels for 1%

profile of v7, /device:TPU:1, one launch (start us, length us, event | category | flops | bytes accessed | tf_op | source)
XLA Modules:
  0.0 105.4 jit_solution(14779830726838846324)
XLA Ops:
  0.6 0.0 copy-start
  0.6 0.0 copy-start.1
  0.7 2.4 %shard_map.104 = (bf16[512,256]{1,0:T(8,128)(2,1)}, bf16[32,256]{1,0:T(8,128)(2,1)}, bf16[32,256]{1,0:T(8,128)(2,1)}, bf16[32,256]{1,0:T(8,128)(2,1)}, bf16[32,256]{1,0:T(8,128)(2,1)}) custom-call(bf16[1024,256]{1,0:T(8,128)(2,1)} %features_ref.3, s32[4,128]{1,0:T(4,128)} %bitcast.12, s32[1,128]{1,0:T(1,128)} %bitcast.13), custom_call_target="tpu_custom_call" | custom-call | tf_op jit(solution)/shard_map/pallas_call | solution.py:231
  3.1 19.1 %all-to-all-start = ((bf16[64,8,256]{2,1,0:T(8,128)(2,1)}), bf16[64,8,256]{2,1,0:T(8,128)(2,1)S(1)}, u32[]{:S(2)}, u32[]{:S(2)}) async-start(bf16[64,8,256]{2,1,0:T(8,128)(2,1)} %bitcast.11), calls=%async_computation | async-start | bytes 524288 | tf_op jit(solution)/shard_map/all_to_all | solution.py:359
  22.2 0.7 pad_maximum_fusion
  22.9 3.3 %collective-permute-start = (bf16[64,256]{1,0:T(8,128)(2,1)S(1)}, bf16[64,256]{1,0:T(8,128)(2,1)S(1)}, u32[]{:S(2)}, u32[]{:S(2)}) collective-permute-start(bf16[64,256]{1,0:T(8,128)(2,1)S(1)} %pad_maximum_fusion), channel_id=1, source_target_pairs={{0,1},{1,2},{2,3},{3,0},{4,5},{5,6},{6,7},{7,4},{8,9},{9,10},{10,1... | collective-permute-start | bytes 98312 | tf_op jit(solution)/shard_map/ppermute | solution.py:362
  26.3 3.0 %collective-permute-done = bf16[64,256]{1,0:T(8,128)(2,1)S(1)} collective-permute-done((bf16[64,256]{1,0:T(8,128)(2,1)S(1)}, bf16[64,256]{1,0:T(8,128)(2,1)S(1)}, u32[]{:S(2)}, u32[]{:S(2)}) %collective-permute-start) | collective-permute-done | bytes 32800 | tf_op jit(solution)/shard_map/ppermute | solution.py:362
  29.3 0.0 copy-done.8
  29.3 0.0 copy-start.5
  29.3 0.0 copy-start.6
  29.3 0.0 copy-start.7
  29.4 3.5 %collective-permute-start.1 = (bf16[64,256]{1,0:T(8,128)(2,1)S(1)}, bf16[64,256]{1,0:T(8,128)(2,1)S(1)}, u32[]{:S(2)}, u32[]{:S(2)}) collective-permute-start(bf16[64,256]{1,0:T(8,128)(2,1)S(1)} %pad_maximum_fusion.1), channel_id=1, source_target_pairs={{0,2},{1,3},{2,0},{3,1},{4,6},{5,7},{6,4},{7,5},{8,10},{9,11},{10,... | collective-permute-start | bytes 98312 | tf_op jit(solution)/shard_map/ppermute | solution.py:363
  32.9 0.0 copy-done
  32.9 0.0 copy-done.1
  32.9 0.0 copy-done.4
  32.9 0.0 copy-done.5
  32.9 0.0 copy-done.6
  33.0 0.0 copy-start.2
  33.0 1.6 %shard_map.105 = (f32[1024,256]{1,0:T(8,128)S(1)}, f32[8,128]{1,0:T(8,128)S(1)}) custom-call(s32[16]{0:T(128)S(1)} %copy-done.4, s32[8]{0:T(128)S(1)} %copy-done.7, s32[8]{0:T(128)S(1)} %copy-done.5, s32[1,2]{1,0:T(1,128)S(1)} %copy-done.6, bf16[1024,256]{1,0:T(8,128)(2,1)S(1)} %copy-done, bf16[16,128,128]{2,1,0:T(8,128)(2,1)S(1)} %copy-done.1), custom_call_target="tpu_custom_call" | custom-call | flops 100000000 | bytes 2000000 | tf_op jit(solution)/shard_map/pallas_call | solution.py:271
  34.5 1.3 %collective-permute-done.1 = bf16[64,256]{1,0:T(8,128)(2,1)S(1)} collective-permute-done((bf16[64,256]{1,0:T(8,128)(2,1)S(1)}, bf16[64,256]{1,0:T(8,128)(2,1)S(1)}, u32[]{:S(2)}, u32[]{:S(2)}) %collective-permute-start.1) | collective-permute-done | bytes 32800 | tf_op jit(solution)/shard_map/ppermute | solution.py:363
  35.8 5.4 %all-to-all-done = bf16[64,8,256]{2,1,0:T(8,128)(2,1)S(1)} async-done(((bf16[64,8,256]{2,1,0:T(8,128)(2,1)}), bf16[64,8,256]{2,1,0:T(8,128)(2,1)S(1)}, u32[]{:S(2)}, u32[]{:S(2)}) %all-to-all-start) | async-done | bytes 262176 | tf_op jit(solution)/shard_map/all_to_all | solution.py:359
  41.2 4.8 %collective-permute-start.2 = (bf16[512,256]{1,0:T(8,128)(2,1)S(1)}, bf16[512,256]{1,0:T(8,128)(2,1)S(1)}, u32[]{:S(2)}, u32[]{:S(2)}) collective-permute-start(bf16[512,256]{1,0:T(8,128)(2,1)S(1)} %bitcast.8), channel_id=1, source_target_pairs={{0,4},{4,0},{1,5},{5,1},{2,6},{6,2},{3,7},{7,3},{8,12},{12,8},{9,1... | collective-permute-start | bytes 786440 | tf_op jit(solution)/shard_map/ppermute | solution.py:367
  46.0 1.1 %collective-permute-done.2.crossed_ref = bf16[512,256]{1,0:T(8,128)(2,1)S(1)} collective-permute-done((bf16[512,256]{1,0:T(8,128)(2,1)S(1)}, bf16[512,256]{1,0:T(8,128)(2,1)S(1)}, u32[]{:S(2)}, u32[]{:S(2)}) %collective-permute-start.2) | collective-permute-done | bytes 262176 | tf_op jit(solution)/shard_map/ppermute | solution.py:367
  47.2 1.8 %shard_map.106 = (bf16[1024,256]{1,0:T(8,128)(2,1)S(1)}, f32[544,128]{1,0:T(8,128)S(1)}) custom-call(s32[16]{0:T(128)S(1)} %copy-done.4, s32[8]{0:T(128)S(1)} %copy-done.5, s32[1,2]{1,0:T(1,128)S(1)} %copy-done.6, bf16[1024,256]{1,0:T(8,128)(2,1)S(1)} %copy-done, bf16[512,256]{1,0:T(8,128)(2,1)S(1)} %bitcast.9, ...), custom_call_target="tpu_custom_call" | custom-call | tf_op jit(solution)/shard_map/pallas_call | solution.py:327
  49.0 16.2 %all_to_all.20 = f32[32,1,2176]{2,1,0:T(1,128)S(1)} all-to-all(f32[32,1,2176]{2,1,0:T(1,128)S(1)} %bitcast.10), channel_id=1, replica_groups=mesh['x'=4,'z'=16,'c'=2,'y'=4] {'x','c','y'}, dimensions={0} | all-to-all | bytes 557056 | tf_op jit(solution)/shard_map/all_to_all | solution.py:346
  65.2 0.2 reduce_sum.18
  65.4 0.1 broadcast_in_dim.4
  65.5 16.4 %all_to_all.21 = f32[16,1,2176]{2,1,0:T(1,128)S(1)} all-to-all(f32[16,1,2176]{2,1,0:T(1,128)S(1)} %broadcast_in_dim.4), channel_id=1, replica_groups=mesh['x'=4,'z'=16,'c'=2,'y'=4] {'z'}, dimensions={0} | all-to-all | bytes 278528 | tf_op jit(solution)/shard_map/all_to_all | solution.py:348
  81.9 0.1 reduce_sum.19
  82.0 0.1 broadcast_in_dim.5
  82.2 15.8 %all_to_all.22 = f32[32,1,2176]{2,1,0:T(1,128)S(1)} all-to-all(f32[32,1,2176]{2,1,0:T(1,128)S(1)} %broadcast_in_dim.5), channel_id=1, replica_groups=mesh['x'=4,'z'=16,'c'=2,'y'=4] {'x','c','y'}, dimensions={0} | all-to-all | bytes 557056 | tf_op jit(solution)/shard_map/all_to_all | solution.py:350
  98.0 7.4 %shard_map.107 = (bf16[1024,256]{1,0:T(8,128)(2,1)}, f32[1,1]{1,0:T(1,128)}) custom-call(f32[544,128]{1,0:T(8,128)S(1)} %bitcast.7, bf16[1024,256]{1,0:T(8,128)(2,1)S(1)} %get-tuple-element.35.hidden_ref), custom_call_target="tpu_custom_call" | custom-call | tf_op jit(solution)/shard_map/pallas_call | solution.py:154
  (9 shorter events, 0.0 us)
Async XLA Ops:
  0.6 32.3 %copy-start = (bf16[1024,256]{1,0:T(8,128)(2,1)S(1)}, bf16[1024,256]{1,0:T(8,128)(2,1)}, u32[]{:S(2)}) copy-start(bf16[1024,256]{1,0:T(8,128)(2,1)} %features_ref.3) | copy-start | bytes 1572868
  0.6 32.3 %copy-start.1 = (bf16[16,128,128]{2,1,0:T(8,128)(2,1)S(1)}, bf16[16,128,128]{2,1,0:T(8,128)(2,1)}, u32[]{:S(2)}) copy-start(bf16[16,128,128]{2,1,0:T(8,128)(2,1)} %tile_ref.3) | copy-start | bytes 1572868
  3.1 38.2 %all-to-all-start = ((bf16[64,8,256]{2,1,0:T(8,128)(2,1)}), bf16[64,8,256]{2,1,0:T(8,128)(2,1)S(1)}, u32[]{:S(2)}, u32[]{:S(2)}) async-start(bf16[64,8,256]{2,1,0:T(8,128)(2,1)} %bitcast.11), calls=%async_computation | async-start | bytes 524288 | tf_op jit(solution)/shard_map/all_to_all | solution.py:359
  22.9 6.4 %copy-start.8 = (bf16[32,256]{1,0:T(8,128)(2,1)S(1)}, bf16[32,256]{1,0:T(8,128)(2,1)}, u32[]{:S(2)}) copy-start(bf16[32,256]{1,0:T(8,128)(2,1)} %get-tuple-element.24) | copy-start | bytes 49156
  22.9 6.4 %collective-permute-start = (bf16[64,256]{1,0:T(8,128)(2,1)S(1)}, bf16[64,256]{1,0:T(8,128)(2,1)S(1)}, u32[]{:S(2)}, u32[]{:S(2)}) collective-permute-start(bf16[64,256]{1,0:T(8,128)(2,1)S(1)} %pad_maximum_fusion), channel_id=1, source_target_pairs={{0,1},{1,2},{2,3},{3,0},{4,5},{5,6},{6,7},{7,4},{8,9},{9,10},{10,1... | collective-permute-start | bytes 98312 | tf_op jit(solution)/shard_map/ppermute | solution.py:362
  29.3 3.6 %copy-start.4 = (s32[16]{0:T(128)S(1)}, s32[16]{0:T(128)}, u32[]{:S(2)}) copy-start(s32[16]{0:T(128)} %dst_ref.3) | copy-start | bytes 196
  29.3 3.6 %copy-start.5 = (s32[8]{0:T(128)S(1)}, s32[8]{0:T(128)}, u32[]{:S(2)}) copy-start(s32[8]{0:T(128)} %outer_ref.3) | copy-start | bytes 100
  29.3 3.6 %copy-start.6 = (s32[1,2]{1,0:T(1,128)S(1)}, s32[1,2]{1,0:T(1,128)}, u32[]{:S(2)}) copy-start(s32[1,2]{1,0:T(1,128)} %live_ref.3) | copy-start | bytes 28
  29.3 3.6 %copy-start.7 = (s32[8]{0:T(128)S(1)}, s32[8]{0:T(128)}, u32[]{:S(2)}) copy-start(s32[8]{0:T(128)} %inner_ref.1) | copy-start | bytes 100
  29.4 6.5 %collective-permute-start.1 = (bf16[64,256]{1,0:T(8,128)(2,1)S(1)}, bf16[64,256]{1,0:T(8,128)(2,1)S(1)}, u32[]{:S(2)}, u32[]{:S(2)}) collective-permute-start(bf16[64,256]{1,0:T(8,128)(2,1)S(1)} %pad_maximum_fusion.1), channel_id=1, source_target_pairs={{0,2},{1,3},{2,0},{3,1},{4,6},{5,7},{6,4},{7,5},{8,10},{9,11},{10,... | collective-permute-start | bytes 98312 | tf_op jit(solution)/shard_map/ppermute | solution.py:363
  33.0 14.2 %copy-start.2 = (bf16[256,256]{1,0:T(8,128)(2,1)S(1)}, bf16[256,256]{1,0:T(8,128)(2,1)}, u32[]{:S(2)}) copy-start(bf16[256,256]{1,0:T(8,128)(2,1)} %weight_ref.1) | copy-start | bytes 393220
  35.8 11.4 %copy-start.3 = (bf16[32,256]{1,0:T(8,128)(2,1)S(1)}, bf16[32,256]{1,0:T(8,128)(2,1)}, u32[]{:S(2)}) copy-start(bf16[32,256]{1,0:T(8,128)(2,1)} %get-tuple-element.30.rest_0_) | copy-start | bytes 49156
  41.2 5.9 %collective-permute-start.2 = (bf16[512,256]{1,0:T(8,128)(2,1)S(1)}, bf16[512,256]{1,0:T(8,128)(2,1)S(1)}, u32[]{:S(2)}, u32[]{:S(2)}) collective-permute-start(bf16[512,256]{1,0:T(8,128)(2,1)S(1)} %bitcast.8), channel_id=1, source_target_pairs={{0,4},{4,0},{1,5},{5,1},{2,6},{6,2},{3,7},{7,3},{8,12},{12,8},{9,1... | collective-permute-start | bytes 786440 | tf_op jit(solution)/shard_map/ppermute | solution.py:367
